TPU v7x, 32 devices: a whole 2x2x4 slice. The times are simulated.
32 devices in a mesh: wide: 8 (over z, x), narrow: 4 (over y, core).
Axes of the slice: x: 2, y: 2, z: 4, core: 2. Of those that a mesh axis runs over, the one named last changes fastest.
Arguments:
- cube: bfloat16 [128, 384, 224], P('narrow', 'wide')
Outputs:
- restored: bfloat16 [128, 384, 224], P('narrow', 'wide')
- projector: float32 [224, 224], replicated
All inputs are finite; a program needn't handle non-finite values.
Results may differ from a plain program's by a relative error of at most 0.0034.
Values may be sent and summed in bfloat16 or wider, within the bound.
No kernel may reach another device: no remote copies, remote signals or barrier semaphores. Data moves between devices by JAX's collectives and lax.ppermute only.
A program may use at most 64 MiB of HBM per device.

v0:
```python
import functools

import jax
import jax.numpy as jnp
import numpy as np
from jax import lax
from jax.experimental import pallas as pl
from jax.experimental.pallas import tpu as pltpu
from jax.sharding import PartitionSpec as P

BANDS = 224
RANK = 16
POWER_ITERS = 4
TV_ITERS = 3
LANES = 256
HALF = 128
TAIL = BANDS - HALF
SIDE = 8
SUB = 8
BLOCK = 8
FIT_ROWS = (2, 6, 8, 8, 8)
AHEAD = 4
TV_ROWS = (12, 16)
OUT_ROWS = 4

f32 = jnp.float32
bf16 = jnp.bfloat16


def iotas(shape):
    return lax.broadcasted_iota(jnp.int32, shape, 0), lax.broadcasted_iota(jnp.int32, shape, 1)


def gram_kernel(cube_ref, packed_ref, block, full, sems):
    rows, cols, bands = cube_ref.shape
    pieces = sems.shape[0]
    high = rows // pieces

    def copy(n):
        part = pl.ds(n * high, high)
        return pltpu.make_async_copy(cube_ref.at[part], block.at[part], sems.at[n])

    for n in range(pieces):
        copy(n).start()
    full[HALF:, HALF:] = jnp.zeros((LANES - HALF, LANES - HALF), f32)
    total = None
    for n in range(pieces):
        copy(n).wait()
        flat = block[n * high : (n + 1) * high].reshape(high * cols, bands)
        term = lax.dot_general(flat, flat, (((0,), (0,)), ((), ())), preferred_element_type=f32)
        total = term if total is None else total + term
    full[0:bands, 0:bands] = total
    i, j = iotas((HALF, HALF))
    first = full[0:HALF, 0:HALF]
    second = pltpu.roll(full[HALF:LANES, HALF:LANES], 1, 1)
    packed_ref[0:HALF, :] = jnp.where(j <= i, first, second)
    packed_ref[HALF:bands, :] = full[HALF:bands, 0:HALF]
    if packed_ref.shape[0] > bands:
        packed_ref[bands:, :] = jnp.zeros((packed_ref.shape[0] - bands, HALF), f32)


def sum_kernel(count, pieces_ref, spread_ref):
    high = pieces_ref.shape[0] // count
    parts = [pieces_ref[n * high : (n + 1) * high, :] for n in range(count)]
    total = functools.reduce(jnp.add, parts)
    for n in range(count):
        spread_ref[n * high : (n + 1) * high, :] = total


def split3(x):
    high = x.astype(bf16)
    rest = x - high.astype(f32)
    mid = rest.astype(bf16)
    low = (rest - mid.astype(f32)).astype(bf16)
    return high, mid, low


def product(left, right, dims):
    def dot(a, b):
        return lax.dot_general(a, b, (dims, ((), ())), preferred_element_type=f32)

    n = left[0].shape[0]
    top = dot(jnp.concatenate(left, axis=0), right[0])
    middle = dot(jnp.concatenate(left[:2], axis=0), right[1])
    small = top[2 * n : 3 * n] + middle[n : 2 * n]
    if len(right) > 2:
        small = small + dot(left[0], right[2])
    return top[:n] + ((top[n : 2 * n] + middle[:n]) + small)


def unpack(packed, scale):
    i, j = iotas((HALF, HALF))
    merged = packed[0:HALF, :] * scale
    below = packed[HALF:BANDS, :] * scale
    below = jnp.concatenate([below, jnp.zeros((LANES - BANDS, HALF), f32)], axis=0)
    first = jnp.where(j <= i, merged, 0.0) + jnp.where(j < i, merged, 0.0).T
    moved = pltpu.roll(merged, HALF - 1, 1)
    inside = (i < TAIL) & (j < TAIL)
    second = jnp.where(inside & (j >= i), moved, 0.0) + jnp.where(inside & (j > i), moved, 0.0).T
    return jnp.concatenate(
        [
            jnp.concatenate([first, below.T], axis=1),
            jnp.concatenate([below, second], axis=1),
        ],
        axis=0,
    )


def orthonormal(grown, inner):
    row = lax.broadcasted_iota(jnp.int32, (RANK, HALF), 0)
    work = [
        jnp.concatenate([inner, jnp.zeros((RANK, HALF - RANK), f32)], axis=1),
        grown[:, :HALF],
        grown[:, HALF:],
    ]
    diagonal = jnp.ones((RANK, HALF), f32)
    for k in range(0, RANK, BLOCK):
        columns = [
            jnp.broadcast_to(work[0][:, k + c : k + c + 1], (RANK, HALF)) for c in range(BLOCK)
        ]
        tops = [[part[k + r : k + r + 1, :] for part in work] for r in range(BLOCK)]
        small = [
            [columns[c][k + r : k + r + 1, :] for c in range(r + 1)] for r in range(BLOCK)
        ]
        factors = []
        for j in range(BLOCK):
            pivot = small[j][j]
            inverse = 1.0 / pivot
            diagonal = jnp.where(row == k + j, pivot, diagonal)
            factor = jnp.where(row > k + j, columns[j] * inverse, 0.0)
            factors.append(factor)
            below = [small[i][j] for i in range(BLOCK) if i > j]
            for i in range(j + 1, BLOCK):
                ratio = small[i][j] * inverse
                for c in range(j + 1, i + 1):
                    small[i][c] = small[i][c] - ratio * below[c - j - 1]
                tops[i] = [x - ratio * y for x, y in zip(tops[i], tops[j])]
                columns[i] = columns[i] - factor * below[i - j - 1]
        for n in range(len(work)):
            if n > 0 or k + BLOCK < RANK:
                for j in range(BLOCK):
                    work[n] = work[n] - factors[j] * tops[j][n]
    scale = lax.rsqrt(diagonal)
    return jnp.concatenate([work[1] * scale, work[2] * scale], axis=1)


def subspace(gram, start, held):
    for n, part in enumerate(split3(gram)[:2]):
        held[n] = part

    def times_gram(pieces):
        return product(pieces, [held[0], held[1]], ((1,), (0,)))

    def iterate(_, grown):
        pieces = split3(grown)
        inner = product(pieces, pieces, ((1,), (1,)))
        return orthonormal(times_gram(pieces), inner)

    grown = lax.fori_loop(0, POWER_ITERS - 1, iterate, times_gram(split3(start)))
    pieces = split3(grown)
    return orthonormal(grown, product(pieces, pieces, ((1,), (1,))))


def halo_kernel(depth, left_ref, right_ref, top_ref, bottom_ref, up_ref, down_ref, side_ref, wide):
    rows, cols = side_ref.shape[0], top_ref.shape[1]
    wide[...] = jnp.zeros_like(wide)
    wide[:, 0:depth] = right_ref[...].astype(f32)
    wide[:, SIDE - depth :] = left_ref[...].astype(f32)
    side = wide[...].astype(bf16)
    side_ref[...] = side
    up_ref[:, 0:cols] = top_ref[...]
    up_ref[:, cols:] = side[:depth]
    down_ref[:, 0:cols] = bottom_ref[...]
    down_ref[:, cols:] = side[rows - depth :]


def subspace_kernel(inv_count, packed_ref, start_ref, basis_ref, held):
    basis_ref[...] = subspace(unpack(packed_ref[...], inv_count), start_ref[...], held)


def main_kernel(
    depth, n_rows, n_cols, basis_ref, mid_ref, above_ref, below_ref, side_ref,
    out_ref, proj_ref, fit, field_a, field_b, out_stage, proj_stage, out_sems, proj_sem
):
    rows, cols, bands = mid_ref.shape
    span = cols + SIDE
    proj_copy = pltpu.make_async_copy(proj_stage, proj_ref, proj_sem)

    def out_copy(n):
        part = pl.ds(n * OUT_ROWS, OUT_ROWS)
        return pltpu.make_async_copy(out_stage.at[part], out_ref.at[part], out_sems.at[n])

    high, mid, low = split3(basis_ref[...])
    tn = (((0,), (0,)), ((), ()))
    mixed = lax.dot_general(
        jnp.concatenate([high, high, high], axis=0),
        jnp.concatenate([high, mid, low], axis=0),
        tn,
        preferred_element_type=f32,
    )
    mixed = mixed * 4.0
    mixed_high = mixed.astype(bf16)
    mixed_low = (mixed - mixed_high.astype(f32)).astype(bf16)
    mixed_both = jnp.concatenate([mixed_high, mixed_low], axis=0)

    def fitted(flat):
        padded = jnp.concatenate([flat, jnp.zeros((flat.shape[0], LANES - bands), bf16)], axis=1)
        both = jnp.concatenate([padded, padded], axis=1)
        return jnp.dot(both, mixed_both, preferred_element_type=f32)

    def project():
        right = jnp.concatenate([high, high, high, mid, mid, low], axis=0)
        left = jnp.concatenate([high, mid, low, high, mid, high], axis=0)
        full = lax.dot_general(left, right, tn, preferred_element_type=f32)
        proj_stage[...] = full[:bands, :bands]
        proj_copy.start()

    def fit_rows(start, stop):
        n = stop - start
        if depth <= start < depth + rows:
            part = slice(start - depth, stop - depth)
            center = mid_ref[part].reshape(n * cols, bands)
            side = side_ref[part].astype(f32).reshape(n * SIDE, bands).astype(bf16)
            res = fitted(jnp.concatenate([center, side], axis=0))
            for h, lane in enumerate(lanes):
                fit[h, start:stop, 0:cols] = res[: n * cols, lane].reshape(n, cols, HALF)
                fit[h, start:stop, cols:span] = res[n * cols :, lane].reshape(n, SIDE, HALF)
        else:
            block = above_ref[...] if start < depth else below_ref[...]
            flat = block.astype(f32).reshape(n * span, bands).astype(bf16)
            res = fitted(flat)
            for h, lane in enumerate(lanes):
                fit[h, start:stop] = res[:, lane].reshape(n, span, HALF)

    row, col = lax.axis_index("narrow"), lax.axis_index("wide")
    at_top, at_bottom = row == 0, row == n_rows - 1
    at_left, at_right = col == 0, col == n_cols - 1
    per = span // SUB
    place = lax.broadcasted_iota(jnp.int32, (SUB, HALF), 0)
    keeps = {}
    for column, shut in ((cols - 1, at_right), (span - 1, at_left)):
        keep = jnp.where((place == column // per) & shut, 0.0, 1.0).astype(f32)
        keeps[column % per] = keeps[column % per] * keep if column % per in keeps else keep
    open_rows = {
        depth - 1: jnp.where(at_top, 0.0, 1.0),
        depth + rows - 1: jnp.where(at_bottom, 0.0, 1.0),
    }
    lanes = [slice(0, HALF), slice(HALF, LANES)]
    fields = [fit, field_a, field_b]

    def natural(ref, h, r):
        return [ref[h, r, pl.ds(w, SUB, stride=per), :] for w in range(per)]

    def spread(ref, h, r):
        return [ref[h, r, w * SUB : (w + 1) * SUB, :] for w in range(per)]

    def slopes(now, later, open_row=None):
        follow = now[1:] + [pltpu.roll(now[0], SUB - 1, 0)]
        downs, acrosses = [], []
        for w in range(per):
            down = later[w] - now[w]
            if open_row is not None:
                down = down * open_row
            across = follow[w] - now[w]
            if w in keeps:
                across = across * keeps[w]
            inverse = lax.rsqrt(down * down + (across * across + 4.0))
            downs.append(down * inverse)
            acrosses.append(across * inverse)
        return downs, acrosses

    def advance(base, before, down, across):
        behind = [pltpu.roll(across[-1], 1, 0)] + across[:-1]
        return [
            base[w] + ((down[w] - before[w]) + (across[w] - behind[w])) for w in range(per)
        ]

    def put(ref, h, r, value):
        for w in range(per):
            ref[h, r, w * SUB : (w + 1) * SUB, :] = value[w]

    tall = rows + 2 * depth
    groups = [(0, depth)]
    for n in FIT_ROWS:
        groups.append((groups[-1][1], groups[-1][1] + n))
    groups += [(depth + rows, tall)]
    ready = 0
    befores = [None] * len(lanes)
    for r in range(tall - 1):
        while ready < len(groups) and groups[ready][0] <= r + 1 + AHEAD:
            fit_rows(*groups[ready])
            ready += 1
            if ready == 4:
                project()
        for h in range(len(lanes)):
            now = natural(fit, h, r)
            down, across = slopes(now, natural(fit, h, r + 1), open_rows.get(r))
            if r > 0:
                put(field_a, h, r, advance(now, befores[h], down, across))
            befores[h] = down

    def step(s, first, trips, unroll):
        source, final = fields[s], s == TV_ITERS - 1

        @pl.when(at_top)
        def _():
            source[:, depth - 1] = source[:, depth]

        @pl.when(at_bottom)
        def _():
            source[:, depth + rows] = source[:, depth + rows - 1]

        def block_step(n, carry):
            carry = list(carry)
            for inner in range(unroll):
                r = first + n * unroll + inner
                for h, lane in enumerate(lanes):
                    now, before = carry[2 * h], carry[2 * h + 1]
                    later = spread(source, h, r + 1)
                    down, across = slopes(now, later)
                    base = [0.5 * (x + y) for x, y in zip(now, natural(fit, h, r))]
                    value = advance(base, before, down, across)
                    if final:
                        for w in range(per):
                            field_a[h, r, pl.ds(w, SUB, stride=per), :] = value[w]
                        result = (field_a[h, r, 0:cols, :] * 0.25).astype(bf16)
                        width = min(lane.stop, bands) - lane.start
                        out_stage[r - depth, :, lane.start : lane.start + width] = result[:, :width]
                    else:
                        put(fields[s + 1], h, r, value)
                    carry[2 * h], carry[2 * h + 1] = later, down
                if final and inner % OUT_ROWS == OUT_ROWS - 1:
                    out_copy(n * (unroll // OUT_ROWS) + inner // OUT_ROWS).start()
            return tuple(carry)

        carry = []
        for h in range(len(lanes)):
            before, now = spread(source, h, first - 1), spread(source, h, first)
            carry += [now, slopes(before, now)[0]]
        lax.fori_loop(0, trips, block_step, tuple(carry))

    step(1, 1, (rows + 4) // TV_ROWS[0], TV_ROWS[0])
    step(2, depth, rows // TV_ROWS[1], TV_ROWS[1])
    proj_copy.wait()
    for n in range(rows // OUT_ROWS):
        out_copy(n).wait()


def start_basis():
    bands = np.arange(BANDS, dtype=np.float32)[None, :]
    cols = np.arange(RANK, dtype=np.float32)[:, None]
    angle = np.float32(np.pi) * (bands + np.float32(0.5)) * cols / np.float32(BANDS)
    return np.pad(np.cos(angle).astype(np.float32), ((0, 0), (0, LANES - BANDS)))


def neighbours(block, axis, dim, width):
    count = lax.axis_size(axis)
    size = block.shape[dim]
    head = lax.slice_in_dim(block, 0, width, axis=dim)
    tail = lax.slice_in_dim(block, size - width, size, axis=dim)
    before = lax.ppermute(tail, axis, [(i, i + 1) for i in range(count - 1)])
    after = lax.ppermute(head, axis, [(i + 1, i) for i in range(count - 1)])
    return before, after


def exchange(pieces, axes):
    return lax.all_to_all(pieces, axes, split_axis=0, concat_axis=0)


def body(cube):
    n_rows = lax.axis_size("narrow")
    n_cols = lax.axis_size("wide")
    count = n_rows * n_cols
    rows, cols, bands = cube.shape
    depth = TV_ITERS
    axes = ("narrow", "wide")

    tall_packed = -(-bands // count) * count
    left, right = neighbours(cube, "wide", 1, depth)
    pieces = 2 if rows % 2 == 0 else 1
    packed = pl.pallas_call(
        gram_kernel,
        in_specs=[pl.BlockSpec(memory_space=pl.ANY)],
        out_shape=jax.ShapeDtypeStruct((tall_packed, HALF), f32),
        scratch_shapes=[
            pltpu.VMEM(cube.shape, cube.dtype),
            pltpu.VMEM((LANES, LANES), f32),
            pltpu.SemaphoreType.DMA((pieces,)),
        ],
        compiler_params=pltpu.CompilerParams(vmem_limit_bytes=62 * 2**20),
    )(cube)
    vmem = pl.BlockSpec(memory_space=pltpu.VMEM)
    pieces_shape = (count, 1, tall_packed // count * HALF)
    part = exchange(packed.reshape(pieces_shape), axes).reshape(tall_packed, HALF)
    share = pl.pallas_call(
        functools.partial(sum_kernel, count),
        in_specs=[vmem],
        out_specs=vmem,
        out_shape=jax.ShapeDtypeStruct((tall_packed, HALF), f32),
        compiler_params=pltpu.CompilerParams(vmem_limit_bytes=16 * 2**20),
    )(part)
    gathered = exchange(share.reshape(pieces_shape), axes).reshape(tall_packed, HALF)

    tall, span = rows + 2 * depth, cols + SIDE
    up, down, side = pl.pallas_call(
        functools.partial(halo_kernel, depth),
        in_specs=[vmem] * 4,
        out_specs=[vmem] * 3,
        out_shape=[
            jax.ShapeDtypeStruct((depth, span, bands), bf16),
            jax.ShapeDtypeStruct((depth, span, bands), bf16),
            jax.ShapeDtypeStruct((rows, SIDE, bands), bf16),
        ],
        scratch_shapes=[pltpu.VMEM((rows, SIDE, bands), f32)],
        cost_estimate=pl.CostEstimate(flops=2**32, bytes_accessed=2**18, transcendentals=0),
        compiler_params=pltpu.CompilerParams(vmem_limit_bytes=16 * 2**20),
    )(left, right, cube[:depth], cube[rows - depth :])
    above = lax.ppermute(down, "narrow", [(i, i + 1) for i in range(n_rows - 1)])
    below = lax.ppermute(up, "narrow", [(i + 1, i) for i in range(n_rows - 1)])

    inv_count = 1.0 / (count * rows * cols)
    basis = pl.pallas_call(
        functools.partial(subspace_kernel, inv_count),
        in_specs=[vmem] * 2,
        out_specs=vmem,
        out_shape=jax.ShapeDtypeStruct((RANK, LANES), f32),
        scratch_shapes=[pltpu.VMEM((2, LANES, LANES), bf16)],
        cost_estimate=pl.CostEstimate(flops=2**32, bytes_accessed=2**18, transcendentals=0),
        compiler_params=pltpu.CompilerParams(vmem_limit_bytes=16 * 2**20),
    )(gathered, jnp.asarray(start_basis()))
    restored, projector = pl.pallas_call(
        functools.partial(main_kernel, depth, n_rows, n_cols),
        in_specs=[vmem] * 5,
        out_specs=[pl.BlockSpec(memory_space=pl.ANY)] * 2,
        out_shape=[
            jax.ShapeDtypeStruct((rows, cols, bands), bf16),
            jax.ShapeDtypeStruct((bands, bands), f32),
        ],
        scratch_shapes=[pltpu.VMEM((2, tall, span, HALF), f32)] * 3
        + [
            pltpu.VMEM((rows, cols, bands), bf16),
            pltpu.VMEM((bands, bands), f32),
            pltpu.SemaphoreType.DMA((rows // OUT_ROWS,)),
            pltpu.SemaphoreType.DMA,
        ],
        compiler_params=pltpu.CompilerParams(vmem_limit_bytes=48 * 2**20),
    )(basis, cube, above, below, side)
    return restored, projector


def solution(mesh):
    return jax.shard_map(
        body,
        mesh=mesh,
        in_specs=(P("narrow", "wide", None),),
        out_specs=(P("narrow", "wide", None), P()),
        check_vma=False,
    )
```

profile of v0, /device:TPU:0, one launch (start us, length us, event | category | flops | bytes accessed | tf_op | source)
XLA Modules:
  0.0 37.4 jit_solution(9799829099129683288)
XLA Ops:
  0.6 0.0 copy-start
  0.6 2.4 %shard_map.41 = f32[224,128]{1,0:T(8,128)} custom-call(bf16[32,48,224]{2,1,0:T(8,128)(2,1)} %mid_ref.1), custom_call_target="tpu_custom_call" | custom-call | tf_op jit(solution)/shard_map/pallas_call | solution.py:381
  3.0 7.3 %all-to-all-start = ((f32[32,1,896]{2,1,0:T(1,128)}), f32[32,1,896]{2,1,0:T(1,128)S(1)}, u32[]{:S(2)}, u32[]{:S(2)}) async-start(f32[32,1,896]{2,1,0:T(1,128)} %bitcast.6), calls=%async_computation | async-start | bytes 229376 | tf_op jit(solution)/shard_map/all_to_all | solution.py:367
  10.3 0.0 copy-done
  10.3 0.1 fusion.1
  10.4 1.3 %collective-permute-start.1 = (bf16[32,3,224]{2,1,0:T(4,128)(2,1)S(1)}, bf16[32,3,224]{2,1,0:T(4,128)(2,1)S(1)}, u32[]{:S(2)}, u32[]{:S(2)}) collective-permute-start(bf16[32,3,224]{2,1,0:T(4,128)(2,1)S(1)} %get-tuple-element.10), channel_id=1, source_target_pairs={{4,0},{8,4},{12,8},{16,12},{20,16},{24,20},{28,24},{5,1},{9,5},{13... | collective-permute-start | bytes 129032 | tf_op jit(solution)/shard_map/ppermute | solution.py:362
  11.7 4.5 %collective-permute-start = (bf16[32,3,224]{2,1,0:T(4,128)(2,1)S(1)}, bf16[32,3,224]{2,1,0:T(4,128)(2,1)S(1)}, u32[]{:S(2)}, u32[]{:S(2)}) collective-permute-start(bf16[32,3,224]{2,1,0:T(4,128)(2,1)S(1)} %get-tuple-element.11), channel_id=1, source_target_pairs={{0,4},{4,8},{8,12},{12,16},{16,20},{20,24},{24,28},{1,5},{5,9},{9,... | collective-permute-start | bytes 129032 | tf_op jit(solution)/shard_map/ppermute | solution.py:361
  16.3 1.7 %all-to-all-done = f32[32,1,896]{2,1,0:T(1,128)S(1)} async-done(((f32[32,1,896]{2,1,0:T(1,128)}), f32[32,1,896]{2,1,0:T(1,128)S(1)}, u32[]{:S(2)}, u32[]{:S(2)}) %all-to-all-start) | async-done | bytes 114720 | tf_op jit(solution)/shard_map/all_to_all | solution.py:367
  18.0 0.7 %shard_map.42 = f32[224,128]{1,0:T(8,128)} custom-call(f32[224,128]{1,0:T(8,128)S(1)} %bitcast.4), custom_call_target="tpu_custom_call" | custom-call | tf_op jit(solution)/shard_map/pallas_call | solution.py:395
  18.7 4.1 %all-to-all-start.1 = ((f32[32,1,896]{2,1,0:T(1,128)}), f32[32,1,896]{2,1,0:T(1,128)S(1)}, u32[]{:S(2)}, u32[]{:S(2)}) async-start(f32[32,1,896]{2,1,0:T(1,128)} %bitcast.2), calls=%async_computation.1 | async-start | bytes 229376 | tf_op jit(solution)/shard_map/all_to_all | solution.py:367
  22.7 0.0 collective-permute-done.1.right_ref
  22.8 0.0 collective-permute-done.left_ref
  22.8 0.0 copy-start.1
  22.8 0.1 shard_map.44
  22.9 2.2 %collective-permute-start.2 = (bf16[3,56,224]{2,1,0:T(8,128)(2,1)S(1)}, bf16[3,56,224]{2,1,0:T(8,128)(2,1)S(1)}, u32[]{:S(2)}, u32[]{:S(2)}) collective-permute-start(bf16[3,56,224]{2,1,0:T(8,128)(2,1)S(1)} %get-tuple-element.5), channel_id=1, source_target_pairs={{0,1},{1,2},{2,3},{4,5},{5,6},{6,7},{8,9},{9,10},{10,11},{12,13},{... | collective-permute-start | bytes 225800 | tf_op jit(solution)/shard_map/ppermute | solution.py:418
  25.0 1.3 %collective-permute-start.3 = (bf16[3,56,224]{2,1,0:T(8,128)(2,1)S(1)}, bf16[3,56,224]{2,1,0:T(8,128)(2,1)S(1)}, u32[]{:S(2)}, u32[]{:S(2)}) collective-permute-start(bf16[3,56,224]{2,1,0:T(8,128)(2,1)S(1)} %get-tuple-element.6), channel_id=1, source_target_pairs={{1,0},{2,1},{3,2},{5,4},{6,5},{7,6},{9,8},{10,9},{11,10},{13,12},{... | collective-permute-start | bytes 225800 | tf_op jit(solution)/shard_map/ppermute | solution.py:419
  26.3 4.1 %all-to-all-done.1 = f32[32,1,896]{2,1,0:T(1,128)S(1)} async-done(((f32[32,1,896]{2,1,0:T(1,128)}), f32[32,1,896]{2,1,0:T(1,128)S(1)}, u32[]{:S(2)}, u32[]{:S(2)}) %all-to-all-start.1) | async-done | bytes 114720 | tf_op jit(solution)/shard_map/all_to_all | solution.py:367
  30.4 0.0 copy-done.1
  30.4 2.3 %shard_map.43.basis_ref = f32[16,256]{1,0:T(8,128)S(1)} custom-call(f32[224,128]{1,0:T(8,128)S(1)} %bitcast.5, f32[16,256]{1,0:T(8,128)S(1)} %copy-done.1), custom_call_target="tpu_custom_call" | custom-call | flops 4294967296 | bytes 262144 | tf_op jit(solution)/shard_map/pallas_call | solution.py:422
  32.7 0.0 collective-permute-done.2.above_ref
  32.7 0.0 collective-permute-done.3.below_ref
  32.7 4.7 %shard_map.45 = (bf16[32,48,224]{2,1,0:T(8,128)(2,1)}, f32[224,224]{1,0:T(8,128)}) custom-call(f32[16,256]{1,0:T(8,128)S(1)} %shard_map.43.basis_ref, bf16[32,48,224]{2,1,0:T(8,128)(2,1)S(1)} %copy-done, bf16[3,56,224]{2,1,0:T(8,128)(2,1)S(1)} %collective-permute-done.2.above_ref, bf16[3,56,224]{2,1,0:T(8,128)(2,1)S(1)} %collective-permute-done.3.below_ref, ...), custom_call_target="tpu_custom_call" | custom-call | tf_op jit(solution)/shard_map/pallas_call | solution.py:431
  (1 shorter events, 0.0 us)
Async XLA Ops:
  0.6 9.7 %copy-start = (bf16[32,48,224]{2,1,0:T(8,128)(2,1)S(1)}, bf16[32,48,224]{2,1,0:T(8,128)(2,1)}, u32[]{:S(2)}) copy-start(bf16[32,48,224]{2,1,0:T(8,128)(2,1)} %mid_ref.1) | copy-start | bytes 2064388
  3.0 15.0 %all-to-all-start = ((f32[32,1,896]{2,1,0:T(1,128)}), f32[32,1,896]{2,1,0:T(1,128)S(1)}, u32[]{:S(2)}, u32[]{:S(2)}) async-start(f32[32,1,896]{2,1,0:T(1,128)} %bitcast.6), calls=%async_computation | async-start | bytes 229376 | tf_op jit(solution)/shard_map/all_to_all | solution.py:367
  10.4 12.4 %collective-permute-start.1 = (bf16[32,3,224]{2,1,0:T(4,128)(2,1)S(1)}, bf16[32,3,224]{2,1,0:T(4,128)(2,1)S(1)}, u32[]{:S(2)}, u32[]{:S(2)}) collective-permute-start(bf16[32,3,224]{2,1,0:T(4,128)(2,1)S(1)} %get-tuple-element.10), channel_id=1, source_target_pairs={{4,0},{8,4},{12,8},{16,12},{20,16},{24,20},{28,24},{5,1},{9,5},{13... | collective-permute-start | bytes 129032 | tf_op jit(solution)/shard_map/ppermute | solution.py:362
  11.7 11.1 %collective-permute-start = (bf16[32,3,224]{2,1,0:T(4,128)(2,1)S(1)}, bf16[32,3,224]{2,1,0:T(4,128)(2,1)S(1)}, u32[]{:S(2)}, u32[]{:S(2)}) collective-permute-start(bf16[32,3,224]{2,1,0:T(4,128)(2,1)S(1)} %get-tuple-element.11), channel_id=1, source_target_pairs={{0,4},{4,8},{8,12},{12,16},{16,20},{20,24},{24,28},{1,5},{5,9},{9,... | collective-permute-start | bytes 129032 | tf_op jit(solution)/shard_map/ppermute | solution.py:361
  18.7 11.7 %all-to-all-start.1 = ((f32[32,1,896]{2,1,0:T(1,128)}), f32[32,1,896]{2,1,0:T(1,128)S(1)}, u32[]{:S(2)}, u32[]{:S(2)}) async-start(f32[32,1,896]{2,1,0:T(1,128)} %bitcast.2), calls=%async_computation.1 | async-start | bytes 229376 | tf_op jit(solution)/shard_map/all_to_all | solution.py:367
  22.8 7.6 %copy-start.1 = (f32[16,256]{1,0:T(8,128)S(1)}, f32[16,256]{1,0:T(8,128)}, u32[]{:S(2)}) copy-start(f32[16,256]{1,0:T(8,128)} %constant.2.clone.start_ref) | copy-start | bytes 49156
  22.9 9.8 %collective-permute-start.2 = (bf16[3,56,224]{2,1,0:T(8,128)(2,1)S(1)}, bf16[3,56,224]{2,1,0:T(8,128)(2,1)S(1)}, u32[]{:S(2)}, u32[]{:S(2)}) collective-permute-start(bf16[3,56,224]{2,1,0:T(8,128)(2,1)S(1)} %get-tuple-element.5), channel_id=1, source_target_pairs={{0,1},{1,2},{2,3},{4,5},{5,6},{6,7},{8,9},{9,10},{10,11},{12,13},{... | collective-permute-start | bytes 225800 | tf_op jit(solution)/shard_map/ppermute | solution.py:418
  25.0 7.7 %collective-permute-start.3 = (bf16[3,56,224]{2,1,0:T(8,128)(2,1)S(1)}, bf16[3,56,224]{2,1,0:T(8,128)(2,1)S(1)}, u32[]{:S(2)}, u32[]{:S(2)}) collective-permute-start(bf16[3,56,224]{2,1,0:T(8,128)(2,1)S(1)} %get-tuple-element.6), channel_id=1, source_target_pairs={{1,0},{2,1},{3,2},{5,4},{6,5},{7,6},{9,8},{10,9},{11,10},{13,12},{... | collective-permute-start | bytes 225800 | tf_op jit(solution)/shard_map/ppermute | solution.py:419
where the time goes:
time: 37.7 us; the launch traced here: 37.4 us
  starting transfers between devices  20.7 us (55%)
  Pallas kernels  10.1 us (27%)
  waiting for transfers between devices  5.77 us (15%)
  between operations  0.77 us (2%)
    all_to_all x2, starting transfers between devices, exchange(): return lax.all_to_all(pieces, axes, split_axis=0, concat_axis=0)  11.4 us
    all_to_all x2, waiting for transfers between devices, exchange(): return lax.all_to_all(pieces, axes, split_axis=0, concat_axis=0)  5.76 us
    pallas_call x1, Pallas kernels, body(): pl.pallas_call(functools.partial(main_kernel, depth, n_rows, n_cols), in_...  4.66 us
    ppermute x1, starting transfers between devices, neighbours(): before = lax.ppermute(tail, axis, [(i, i + 1) for i in range(count - 1)])  4.55 us
    pallas_call x1, Pallas kernels, body(): pl.pallas_call(gram_kernel, in_specs=[pl.BlockSpec(memory_space=pl.ANY)],...  2.36 us
    pallas_call x1, Pallas kernels, body(): pl.pallas_call(functools.partial(subspace_kernel, inv_count), in_specs=[v...  2.27 us
    ppermute x1, starting transfers between devices, body(): lax.ppermute(down, 'narrow', [(i, i + 1) for i in range(n_rows - 1)])  2.16 us
    ppermute x1, starting transfers between devices, neighbours(): after = lax.ppermute(head, axis, [(i + 1, i) for i in range(count - 1)])  1.29 us
  transfers between devices with their start and end apart: 6, of which 2 were waited for; matrix products, arithmetic and copies ran while one was open for 0% of the time, Pallas kernels for 8%

commit v1 on v0

--- a/solution.py
+++ b/solution.py
@@ -20,7 +20,7 @@
 BLOCK = 8
 FIT_ROWS = (2, 6, 8, 8, 8)
 AHEAD = 4
-TV_ROWS = (12, 16)
+TV_ROWS = (17, 16)
 OUT_ROWS = 4
 
 f32 = jnp.float32
@@ -125,7 +125,7 @@
         factors = []
         for j in range(BLOCK):
             pivot = small[j][j]
-            inverse = 1.0 / pivot
+            inverse = pl.reciprocal(pivot, full_range=False)
             diagonal = jnp.where(row == k + j, pivot, diagonal)
             factor = jnp.where(row > k + j, columns[j] * inverse, 0.0)
             factors.append(factor)
@@ -339,7 +339,7 @@
             carry += [now, slopes(before, now)[0]]
         lax.fori_loop(0, trips, block_step, tuple(carry))
 
-    step(1, 1, (rows + 4) // TV_ROWS[0], TV_ROWS[0])
+    step(1, 2, (rows + 2) // TV_ROWS[0], TV_ROWS[0])
     step(2, depth, rows // TV_ROWS[1], TV_ROWS[1])
     proj_copy.wait()
     for n in range(rows // OUT_ROWS):
@@ -376,7 +376,6 @@
     axes = ("narrow", "wide")
 
     tall_packed = -(-bands // count) * count
-    left, right = neighbours(cube, "wide", 1, depth)
     pieces = 2 if rows % 2 == 0 else 1
     packed = pl.pallas_call(
         gram_kernel,
@@ -389,6 +388,8 @@
         ],
         compiler_params=pltpu.CompilerParams(vmem_limit_bytes=62 * 2**20),
     )(cube)
+    packed, cube = lax.optimization_barrier((packed, cube))
+    left, right = neighbours(cube, "wide", 1, depth)
     vmem = pl.BlockSpec(memory_space=pltpu.VMEM)
     pieces_shape = (count, 1, tall_packed // count * HALF)
     part = exchange(packed.reshape(pieces_shape), axes).reshape(tall_packed, HALF)

time: 37.7 us -> 37.6 us (level)
  no operation moved by 1% of the time
where the time goes in v1:
time: 37.6 us; the launch traced here: 37.3 us
  starting transfers between devices  20.7 us (55%)
  Pallas kernels  9.99 us (27%)
  waiting for transfers between devices  5.77 us (15%)
  between operations  0.77 us (2%)
    all_to_all x2, starting transfers between devices, exchange(): return lax.all_to_all(pieces, axes, split_axis=0, concat_axis=0)  11.4 us
    all_to_all x2, waiting for transfers between devices, exchange(): return lax.all_to_all(pieces, axes, split_axis=0, concat_axis=0)  5.76 us
    pallas_call x1, Pallas kernels, body(): pl.pallas_call(functools.partial(main_kernel, depth, n_rows, n_cols), in_...  4.59 us
    ppermute x1, starting transfers between devices, neighbours(): before = lax.ppermute(tail, axis, [(i, i + 1) for i in range(count - 1)])  4.55 us
    pallas_call x1, Pallas kernels, body(): pl.pallas_call(gram_kernel, in_specs=[pl.BlockSpec(memory_space=pl.ANY)],...  2.36 us
    pallas_call x1, Pallas kernels, body(): pl.pallas_call(functools.partial(subspace_kernel, inv_count), in_specs=[v...  2.27 us
    ppermute x1, starting transfers between devices, body(): lax.ppermute(down, 'narrow', [(i, i + 1) for i in range(n_rows - 1)])  2.16 us
    ppermute x1, starting transfers between devices, neighbours(): after = lax.ppermute(head, axis, [(i + 1, i) for i in range(count - 1)])  1.29 us
  transfers between devices with their start and end apart: 6, of which 2 were waited for; matrix products, arithmetic and copies ran while one was open for 0% of the time, Pallas kernels for 8%

profile of v1, /device:TPU:0, one launch (start us, length us, event | category | flops | bytes accessed | tf_op | source)
XLA Modules:
  0.0 37.3 jit_solution(7431027704727907189)
XLA Ops:
  0.6 0.0 copy-start
  0.6 2.4 %shard_map.41 = f32[224,128]{1,0:T(8,128)} custom-call(bf16[32,48,224]{2,1,0:T(8,128)(2,1)} %mid_ref), custom_call_target="tpu_custom_call" | custom-call | tf_op jit(solution)/shard_map/pallas_call | solution.py:380
  3.0 7.3 %all-to-all-start = ((f32[32,1,896]{2,1,0:T(1,128)}), f32[32,1,896]{2,1,0:T(1,128)S(1)}, u32[]{:S(2)}, u32[]{:S(2)}) async-start(f32[32,1,896]{2,1,0:T(1,128)} %bitcast.6), calls=%async_computation | async-start | bytes 229376 | tf_op jit(solution)/shard_map/all_to_all | solution.py:367
  10.3 0.0 copy-done
  10.3 0.1 fusion.1
  10.4 1.3 %collective-permute-start.1 = (bf16[32,3,224]{2,1,0:T(4,128)(2,1)S(1)}, bf16[32,3,224]{2,1,0:T(4,128)(2,1)S(1)}, u32[]{:S(2)}, u32[]{:S(2)}) collective-permute-start(bf16[32,3,224]{2,1,0:T(4,128)(2,1)S(1)} %get-tuple-element.14), channel_id=1, source_target_pairs={{4,0},{8,4},{12,8},{16,12},{20,16},{24,20},{28,24},{5,1},{9,5},{13... | collective-permute-start | bytes 129032 | tf_op jit(solution)/shard_map/ppermute | solution.py:362
  11.7 4.5 %collective-permute-start = (bf16[32,3,224]{2,1,0:T(4,128)(2,1)S(1)}, bf16[32,3,224]{2,1,0:T(4,128)(2,1)S(1)}, u32[]{:S(2)}, u32[]{:S(2)}) collective-permute-start(bf16[32,3,224]{2,1,0:T(4,128)(2,1)S(1)} %get-tuple-element.15), channel_id=1, source_target_pairs={{0,4},{4,8},{8,12},{12,16},{16,20},{20,24},{24,28},{1,5},{5,9},{9,... | collective-permute-start | bytes 129032 | tf_op jit(solution)/shard_map/ppermute | solution.py:361
  16.3 1.7 %all-to-all-done = f32[32,1,896]{2,1,0:T(1,128)S(1)} async-done(((f32[32,1,896]{2,1,0:T(1,128)}), f32[32,1,896]{2,1,0:T(1,128)S(1)}, u32[]{:S(2)}, u32[]{:S(2)}) %all-to-all-start) | async-done | bytes 114720 | tf_op jit(solution)/shard_map/all_to_all | solution.py:367
  18.0 0.7 %shard_map.42 = f32[224,128]{1,0:T(8,128)} custom-call(f32[224,128]{1,0:T(8,128)S(1)} %bitcast.4), custom_call_target="tpu_custom_call" | custom-call | tf_op jit(solution)/shard_map/pallas_call | solution.py:396
  18.7 4.1 %all-to-all-start.1 = ((f32[32,1,896]{2,1,0:T(1,128)}), f32[32,1,896]{2,1,0:T(1,128)S(1)}, u32[]{:S(2)}, u32[]{:S(2)}) async-start(f32[32,1,896]{2,1,0:T(1,128)} %bitcast.2), calls=%async_computation.1 | async-start | bytes 229376 | tf_op jit(solution)/shard_map/all_to_all | solution.py:367
  22.7 0.0 collective-permute-done.1.right_ref
  22.8 0.0 collective-permute-done.left_ref
  22.8 0.0 copy-start.1
  22.8 0.1 shard_map.44
  22.9 2.2 %collective-permute-start.2 = (bf16[3,56,224]{2,1,0:T(8,128)(2,1)S(1)}, bf16[3,56,224]{2,1,0:T(8,128)(2,1)S(1)}, u32[]{:S(2)}, u32[]{:S(2)}) collective-permute-start(bf16[3,56,224]{2,1,0:T(8,128)(2,1)S(1)} %get-tuple-element.9), channel_id=1, source_target_pairs={{0,1},{1,2},{2,3},{4,5},{5,6},{6,7},{8,9},{9,10},{10,11},{12,13},{... | collective-permute-start | bytes 225800 | tf_op jit(solution)/shard_map/ppermute | solution.py:419
  25.0 1.3 %collective-permute-start.3 = (bf16[3,56,224]{2,1,0:T(8,128)(2,1)S(1)}, bf16[3,56,224]{2,1,0:T(8,128)(2,1)S(1)}, u32[]{:S(2)}, u32[]{:S(2)}) collective-permute-start(bf16[3,56,224]{2,1,0:T(8,128)(2,1)S(1)} %get-tuple-element.10), channel_id=1, source_target_pairs={{1,0},{2,1},{3,2},{5,4},{6,5},{7,6},{9,8},{10,9},{11,10},{13,12},{... | collective-permute-start | bytes 225800 | tf_op jit(solution)/shard_map/ppermute | solution.py:420
  26.3 4.1 %all-to-all-done.1 = f32[32,1,896]{2,1,0:T(1,128)S(1)} async-done(((f32[32,1,896]{2,1,0:T(1,128)}), f32[32,1,896]{2,1,0:T(1,128)S(1)}, u32[]{:S(2)}, u32[]{:S(2)}) %all-to-all-start.1) | async-done | bytes 114720 | tf_op jit(solution)/shard_map/all_to_all | solution.py:367
  30.4 0.0 copy-done.1
  30.4 2.3 %shard_map.43.basis_ref = f32[16,256]{1,0:T(8,128)S(1)} custom-call(f32[224,128]{1,0:T(8,128)S(1)} %bitcast.5, f32[16,256]{1,0:T(8,128)S(1)} %copy-done.1), custom_call_target="tpu_custom_call" | custom-call | flops 4294967296 | bytes 262144 | tf_op jit(solution)/shard_map/pallas_call | solution.py:423
  32.7 0.0 collective-permute-done.2.above_ref
  32.7 0.0 collective-permute-done.3.below_ref
  32.7 4.6 %shard_map.45 = (bf16[32,48,224]{2,1,0:T(8,128)(2,1)}, f32[224,224]{1,0:T(8,128)}) custom-call(f32[16,256]{1,0:T(8,128)S(1)} %shard_map.43.basis_ref, bf16[32,48,224]{2,1,0:T(8,128)(2,1)S(1)} %copy-done, bf16[3,56,224]{2,1,0:T(8,128)(2,1)S(1)} %collective-permute-done.2.above_ref, bf16[3,56,224]{2,1,0:T(8,128)(2,1)S(1)} %collective-permute-done.3.below_ref, ...), custom_call_target="tpu_custom_call" | custom-call | tf_op jit(solution)/shard_map/pallas_call | solution.py:432
  (1 shorter events, 0.0 us)
Async XLA Ops:
  0.6 9.7 %copy-start = (bf16[32,48,224]{2,1,0:T(8,128)(2,1)S(1)}, bf16[32,48,224]{2,1,0:T(8,128)(2,1)}, u32[]{:S(2)}) copy-start(bf16[32,48,224]{2,1,0:T(8,128)(2,1)} %mid_ref) | copy-start | bytes 2064388
  3.0 15.0 %all-to-all-start = ((f32[32,1,896]{2,1,0:T(1,128)}), f32[32,1,896]{2,1,0:T(1,128)S(1)}, u32[]{:S(2)}, u32[]{:S(2)}) async-start(f32[32,1,896]{2,1,0:T(1,128)} %bitcast.6), calls=%async_computation | async-start | bytes 229376 | tf_op jit(solution)/shard_map/all_to_all | solution.py:367
  10.4 12.4 %collective-permute-start.1 = (bf16[32,3,224]{2,1,0:T(4,128)(2,1)S(1)}, bf16[32,3,224]{2,1,0:T(4,128)(2,1)S(1)}, u32[]{:S(2)}, u32[]{:S(2)}) collective-permute-start(bf16[32,3,224]{2,1,0:T(4,128)(2,1)S(1)} %get-tuple-element.14), channel_id=1, source_target_pairs={{4,0},{8,4},{12,8},{16,12},{20,16},{24,20},{28,24},{5,1},{9,5},{13... | collective-permute-start | bytes 129032 | tf_op jit(solution)/shard_map/ppermute | solution.py:362
  11.7 11.1 %collective-permute-start = (bf16[32,3,224]{2,1,0:T(4,128)(2,1)S(1)}, bf16[32,3,224]{2,1,0:T(4,128)(2,1)S(1)}, u32[]{:S(2)}, u32[]{:S(2)}) collective-permute-start(bf16[32,3,224]{2,1,0:T(4,128)(2,1)S(1)} %get-tuple-element.15), channel_id=1, source_target_pairs={{0,4},{4,8},{8,12},{12,16},{16,20},{20,24},{24,28},{1,5},{5,9},{9,... | collective-permute-start | bytes 129032 | tf_op jit(solution)/shard_map/ppermute | solution.py:361
  18.7 11.7 %all-to-all-start.1 = ((f32[32,1,896]{2,1,0:T(1,128)}), f32[32,1,896]{2,1,0:T(1,128)S(1)}, u32[]{:S(2)}, u32[]{:S(2)}) async-start(f32[32,1,896]{2,1,0:T(1,128)} %bitcast.2), calls=%async_computation.1 | async-start | bytes 229376 | tf_op jit(solution)/shard_map/all_to_all | solution.py:367
  22.8 7.6 %copy-start.1 = (f32[16,256]{1,0:T(8,128)S(1)}, f32[16,256]{1,0:T(8,128)}, u32[]{:S(2)}) copy-start(f32[16,256]{1,0:T(8,128)} %constant.2.clone.start_ref) | copy-start | bytes 49156
  22.9 9.8 %collective-permute-start.2 = (bf16[3,56,224]{2,1,0:T(8,128)(2,1)S(1)}, bf16[3,56,224]{2,1,0:T(8,128)(2,1)S(1)}, u32[]{:S(2)}, u32[]{:S(2)}) collective-permute-start(bf16[3,56,224]{2,1,0:T(8,128)(2,1)S(1)} %get-tuple-element.9), channel_id=1, source_target_pairs={{0,1},{1,2},{2,3},{4,5},{5,6},{6,7},{8,9},{9,10},{10,11},{12,13},{... | collective-permute-start | bytes 225800 | tf_op jit(solution)/shard_map/ppermute | solution.py:419
  25.0 7.7 %collective-permute-start.3 = (bf16[3,56,224]{2,1,0:T(8,128)(2,1)S(1)}, bf16[3,56,224]{2,1,0:T(8,128)(2,1)S(1)}, u32[]{:S(2)}, u32[]{:S(2)}) collective-permute-start(bf16[3,56,224]{2,1,0:T(8,128)(2,1)S(1)} %get-tuple-element.10), channel_id=1, source_target_pairs={{1,0},{2,1},{3,2},{5,4},{6,5},{7,6},{9,8},{10,9},{11,10},{13,12},{... | collective-permute-start | bytes 225800 | tf_op jit(solution)/shard_map/ppermute | solution.py:420

commit v2 on v1

--- a/solution.py
+++ b/solution.py
@@ -364,7 +364,10 @@
 
 
 def exchange(pieces, axes):
-    return lax.all_to_all(pieces, axes, split_axis=0, concat_axis=0)
+    count = pieces.shape[0]
+    first = lax.axis_size(axes[1]) // 2
+    order = [(n + first) % count for n in range(count)]
+    return lax.all_to_all(pieces, axes, split_axis=0, concat_axis=0, axis_index_groups=[order])
 
 
 def body(cube):

time: 37.6 us -> 37.6 us (level)
  no operation moved by 1% of the time
where the time goes in v2:
time: 37.6 us; the launch traced here: 37.3 us
  starting transfers between devices  20.7 us (55%)
  Pallas kernels  9.99 us (27%)
  waiting for transfers between devices  5.77 us (15%)
  between operations  0.77 us (2%)
    all_to_all x2, starting transfers between devices, exchange(): lax.all_to_all(pieces, axes, split_axis=0, concat_axis=0, axis_index_grou...  11.4 us
    all_to_all x2, waiting for transfers between devices, exchange(): lax.all_to_all(pieces, axes, split_axis=0, concat_axis=0, axis_index_grou...  5.76 us
    pallas_call x1, Pallas kernels, body(): pl.pallas_call(functools.partial(main_kernel, depth, n_rows, n_cols), in_...  4.59 us
    ppermute x1, starting transfers between devices, neighbours(): before = lax.ppermute(tail, axis, [(i, i + 1) for i in range(count - 1)])  4.55 us
    pallas_call x1, Pallas kernels, body(): pl.pallas_call(gram_kernel, in_specs=[pl.BlockSpec(memory_space=pl.ANY)],...  2.36 us
    pallas_call x1, Pallas kernels, body(): pl.pallas_call(functools.partial(subspace_kernel, inv_count), in_specs=[v...  2.27 us
    ppermute x1, starting transfers between devices, body(): lax.ppermute(down, 'narrow', [(i, i + 1) for i in range(n_rows - 1)])  2.16 us
    ppermute x1, starting transfers between devices, neighbours(): after = lax.ppermute(head, axis, [(i + 1, i) for i in range(count - 1)])  1.29 us
  transfers between devices with their start and end apart: 6, of which 2 were waited for; matrix products, arithmetic and copies ran while one was open for 0% of the time, Pallas kernels for 8%

profile of v2, /device:TPU:0, one launch (start us, length us, event | category | flops | bytes accessed | tf_op | source)
XLA Modules:
  0.0 37.3 jit_solution(7257646355180203439)
XLA Ops:
  0.6 0.0 copy-start
  0.6 2.4 %shard_map.41 = f32[224,128]{1,0:T(8,128)} custom-call(bf16[32,48,224]{2,1,0:T(8,128)(2,1)} %mid_ref), custom_call_target="tpu_custom_call" | custom-call | tf_op jit(solution)/shard_map/pallas_call | solution.py:383
  3.0 7.3 %all-to-all-start = ((f32[32,1,896]{2,1,0:T(1,128)}), f32[32,1,896]{2,1,0:T(1,128)S(1)}, u32[]{:S(2)}, u32[]{:S(2)}) async-start(f32[32,1,896]{2,1,0:T(1,128)} %bitcast.6), calls=%async_computation | async-start | bytes 229376 | tf_op jit(solution)/shard_map/all_to_all | solution.py:370
  10.3 0.0 copy-done
  10.3 0.1 fusion.1
  10.4 1.3 %collective-permute-start.1 = (bf16[32,3,224]{2,1,0:T(4,128)(2,1)S(1)}, bf16[32,3,224]{2,1,0:T(4,128)(2,1)S(1)}, u32[]{:S(2)}, u32[]{:S(2)}) collective-permute-start(bf16[32,3,224]{2,1,0:T(4,128)(2,1)S(1)} %get-tuple-element.14), channel_id=1, source_target_pairs={{4,0},{8,4},{12,8},{16,12},{20,16},{24,20},{28,24},{5,1},{9,5},{13... | collective-permute-start | bytes 129032 | tf_op jit(solution)/shard_map/ppermute | solution.py:362
  11.7 4.5 %collective-permute-start = (bf16[32,3,224]{2,1,0:T(4,128)(2,1)S(1)}, bf16[32,3,224]{2,1,0:T(4,128)(2,1)S(1)}, u32[]{:S(2)}, u32[]{:S(2)}) collective-permute-start(bf16[32,3,224]{2,1,0:T(4,128)(2,1)S(1)} %get-tuple-element.15), channel_id=1, source_target_pairs={{0,4},{4,8},{8,12},{12,16},{16,20},{20,24},{24,28},{1,5},{5,9},{9,... | collective-permute-start | bytes 129032 | tf_op jit(solution)/shard_map/ppermute | solution.py:361
  16.3 1.7 %all-to-all-done = f32[32,1,896]{2,1,0:T(1,128)S(1)} async-done(((f32[32,1,896]{2,1,0:T(1,128)}), f32[32,1,896]{2,1,0:T(1,128)S(1)}, u32[]{:S(2)}, u32[]{:S(2)}) %all-to-all-start) | async-done | bytes 114720 | tf_op jit(solution)/shard_map/all_to_all | solution.py:370
  18.0 0.7 %shard_map.42 = f32[224,128]{1,0:T(8,128)} custom-call(f32[224,128]{1,0:T(8,128)S(1)} %bitcast.4), custom_call_target="tpu_custom_call" | custom-call | tf_op jit(solution)/shard_map/pallas_call | solution.py:399
  18.7 4.1 %all-to-all-start.1 = ((f32[32,1,896]{2,1,0:T(1,128)}), f32[32,1,896]{2,1,0:T(1,128)S(1)}, u32[]{:S(2)}, u32[]{:S(2)}) async-start(f32[32,1,896]{2,1,0:T(1,128)} %bitcast.2), calls=%async_computation.1 | async-start | bytes 229376 | tf_op jit(solution)/shard_map/all_to_all | solution.py:370
  22.7 0.0 collective-permute-done.1.right_ref
  22.8 0.0 collective-permute-done.left_ref
  22.8 0.0 copy-start.1
  22.8 0.1 shard_map.44
  22.9 2.2 %collective-permute-start.2 = (bf16[3,56,224]{2,1,0:T(8,128)(2,1)S(1)}, bf16[3,56,224]{2,1,0:T(8,128)(2,1)S(1)}, u32[]{:S(2)}, u32[]{:S(2)}) collective-permute-start(bf16[3,56,224]{2,1,0:T(8,128)(2,1)S(1)} %get-tuple-element.9), channel_id=1, source_target_pairs={{0,1},{1,2},{2,3},{4,5},{5,6},{6,7},{8,9},{9,10},{10,11},{12,13},{... | collective-permute-start | bytes 225800 | tf_op jit(solution)/shard_map/ppermute | solution.py:422
  25.0 1.3 %collective-permute-start.3 = (bf16[3,56,224]{2,1,0:T(8,128)(2,1)S(1)}, bf16[3,56,224]{2,1,0:T(8,128)(2,1)S(1)}, u32[]{:S(2)}, u32[]{:S(2)}) collective-permute-start(bf16[3,56,224]{2,1,0:T(8,128)(2,1)S(1)} %get-tuple-element.10), channel_id=1, source_target_pairs={{1,0},{2,1},{3,2},{5,4},{6,5},{7,6},{9,8},{10,9},{11,10},{13,12},{... | collective-permute-start | bytes 225800 | tf_op jit(solution)/shard_map/ppermute | solution.py:423
  26.3 4.1 %all-to-all-done.1 = f32[32,1,896]{2,1,0:T(1,128)S(1)} async-done(((f32[32,1,896]{2,1,0:T(1,128)}), f32[32,1,896]{2,1,0:T(1,128)S(1)}, u32[]{:S(2)}, u32[]{:S(2)}) %all-to-all-start.1) | async-done | bytes 114720 | tf_op jit(solution)/shard_map/all_to_all | solution.py:370
  30.4 0.0 copy-done.1
  30.4 2.3 %shard_map.43.basis_ref = f32[16,256]{1,0:T(8,128)S(1)} custom-call(f32[224,128]{1,0:T(8,128)S(1)} %bitcast.5, f32[16,256]{1,0:T(8,128)S(1)} %copy-done.1), custom_call_target="tpu_custom_call" | custom-call | flops 4294967296 | bytes 262144 | tf_op jit(solution)/shard_map/pallas_call | solution.py:426
  32.7 0.0 collective-permute-done.2.above_ref
  32.7 0.0 collective-permute-done.3.below_ref
  32.7 4.6 %shard_map.45 = (bf16[32,48,224]{2,1,0:T(8,128)(2,1)}, f32[224,224]{1,0:T(8,128)}) custom-call(f32[16,256]{1,0:T(8,128)S(1)} %shard_map.43.basis_ref, bf16[32,48,224]{2,1,0:T(8,128)(2,1)S(1)} %copy-done, bf16[3,56,224]{2,1,0:T(8,128)(2,1)S(1)} %collective-permute-done.2.above_ref, bf16[3,56,224]{2,1,0:T(8,128)(2,1)S(1)} %collective-permute-done.3.below_ref, ...), custom_call_target="tpu_custom_call" | custom-call | tf_op jit(solution)/shard_map/pallas_call | solution.py:435
  (1 shorter events, 0.0 us)
Async XLA Ops:
  0.6 9.7 %copy-start = (bf16[32,48,224]{2,1,0:T(8,128)(2,1)S(1)}, bf16[32,48,224]{2,1,0:T(8,128)(2,1)}, u32[]{:S(2)}) copy-start(bf16[32,48,224]{2,1,0:T(8,128)(2,1)} %mid_ref) | copy-start | bytes 2064388
  3.0 15.0 %all-to-all-start = ((f32[32,1,896]{2,1,0:T(1,128)}), f32[32,1,896]{2,1,0:T(1,128)S(1)}, u32[]{:S(2)}, u32[]{:S(2)}) async-start(f32[32,1,896]{2,1,0:T(1,128)} %bitcast.6), calls=%async_computation | async-start | bytes 229376 | tf_op jit(solution)/shard_map/all_to_all | solution.py:370
  10.4 12.4 %collective-permute-start.1 = (bf16[32,3,224]{2,1,0:T(4,128)(2,1)S(1)}, bf16[32,3,224]{2,1,0:T(4,128)(2,1)S(1)}, u32[]{:S(2)}, u32[]{:S(2)}) collective-permute-start(bf16[32,3,224]{2,1,0:T(4,128)(2,1)S(1)} %get-tuple-element.14), channel_id=1, source_target_pairs={{4,0},{8,4},{12,8},{16,12},{20,16},{24,20},{28,24},{5,1},{9,5},{13... | collective-permute-start | bytes 129032 | tf_op jit(solution)/shard_map/ppermute | solution.py:362
  11.7 11.1 %collective-permute-start = (bf16[32,3,224]{2,1,0:T(4,128)(2,1)S(1)}, bf16[32,3,224]{2,1,0:T(4,128)(2,1)S(1)}, u32[]{:S(2)}, u32[]{:S(2)}) collective-permute-start(bf16[32,3,224]{2,1,0:T(4,128)(2,1)S(1)} %get-tuple-element.15), channel_id=1, source_target_pairs={{0,4},{4,8},{8,12},{12,16},{16,20},{20,24},{24,28},{1,5},{5,9},{9,... | collective-permute-start | bytes 129032 | tf_op jit(solution)/shard_map/ppermute | solution.py:361
  18.7 11.7 %all-to-all-start.1 = ((f32[32,1,896]{2,1,0:T(1,128)}), f32[32,1,896]{2,1,0:T(1,128)S(1)}, u32[]{:S(2)}, u32[]{:S(2)}) async-start(f32[32,1,896]{2,1,0:T(1,128)} %bitcast.2), calls=%async_computation.1 | async-start | bytes 229376 | tf_op jit(solution)/shard_map/all_to_all | solution.py:370
  22.8 7.6 %copy-start.1 = (f32[16,256]{1,0:T(8,128)S(1)}, f32[16,256]{1,0:T(8,128)}, u32[]{:S(2)}) copy-start(f32[16,256]{1,0:T(8,128)} %constant.2.clone.start_ref) | copy-start | bytes 49156
  22.9 9.8 %collective-permute-start.2 = (bf16[3,56,224]{2,1,0:T(8,128)(2,1)S(1)}, bf16[3,56,224]{2,1,0:T(8,128)(2,1)S(1)}, u32[]{:S(2)}, u32[]{:S(2)}) collective-permute-start(bf16[3,56,224]{2,1,0:T(8,128)(2,1)S(1)} %get-tuple-element.9), channel_id=1, source_target_pairs={{0,1},{1,2},{2,3},{4,5},{5,6},{6,7},{8,9},{9,10},{10,11},{12,13},{... | collective-permute-start | bytes 225800 | tf_op jit(solution)/shard_map/ppermute | solution.py:422
  25.0 7.7 %collective-permute-start.3 = (bf16[3,56,224]{2,1,0:T(8,128)(2,1)S(1)}, bf16[3,56,224]{2,1,0:T(8,128)(2,1)S(1)}, u32[]{:S(2)}, u32[]{:S(2)}) collective-permute-start(bf16[3,56,224]{2,1,0:T(8,128)(2,1)S(1)} %get-tuple-element.10), channel_id=1, source_target_pairs={{1,0},{2,1},{3,2},{5,4},{6,5},{7,6},{9,8},{10,9},{11,10},{13,12},{... | collective-permute-start | bytes 225800 | tf_op jit(solution)/shard_map/ppermute | solution.py:423

commit v3 on v1

--- a/solution.py
+++ b/solution.py
@@ -180,7 +180,7 @@
 
 def main_kernel(
     depth, n_rows, n_cols, basis_ref, mid_ref, above_ref, below_ref, side_ref,
-    out_ref, proj_ref, fit, field_a, field_b, out_stage, proj_stage, out_sems, proj_sem
+    out_ref, proj_ref, fit, half_fit, field_a, field_b, out_stage, proj_stage, out_sems, proj_sem
 ):
     rows, cols, bands = mid_ref.shape
     span = cols + SIDE
@@ -285,7 +285,7 @@
         groups.append((groups[-1][1], groups[-1][1] + n))
     groups += [(depth + rows, tall)]
     ready = 0
-    befores = [None] * len(lanes)
+    befores, nows = [None] * len(lanes), [None] * len(lanes)
     for r in range(tall - 1):
         while ready < len(groups) and groups[ready][0] <= r + 1 + AHEAD:
             fit_rows(*groups[ready])
@@ -293,11 +293,13 @@
             if ready == 4:
                 project()
         for h in range(len(lanes)):
-            now = natural(fit, h, r)
-            down, across = slopes(now, natural(fit, h, r + 1), open_rows.get(r))
+            now = nows[h] if r > 0 else natural(fit, h, r)
+            later = natural(fit, h, r + 1)
+            down, across = slopes(now, later, open_rows.get(r))
             if r > 0:
                 put(field_a, h, r, advance(now, befores[h], down, across))
-            befores[h] = down
+                put(half_fit, h, r, [0.5 * x for x in now])
+            nows[h], befores[h] = later, down
 
     def step(s, first, trips, unroll):
         source, final = fields[s], s == TV_ITERS - 1
@@ -318,7 +320,7 @@
                     now, before = carry[2 * h], carry[2 * h + 1]
                     later = spread(source, h, r + 1)
                     down, across = slopes(now, later)
-                    base = [0.5 * (x + y) for x, y in zip(now, natural(fit, h, r))]
+                    base = [0.5 * x + y for x, y in zip(now, spread(half_fit, h, r))]
                     value = advance(base, before, down, across)
                     if final:
                         for w in range(per):
@@ -437,7 +439,7 @@
             jax.ShapeDtypeStruct((rows, cols, bands), bf16),
             jax.ShapeDtypeStruct((bands, bands), f32),
         ],
-        scratch_shapes=[pltpu.VMEM((2, tall, span, HALF), f32)] * 3
+        scratch_shapes=[pltpu.VMEM((2, tall, span, HALF), f32)] * 4
         + [
             pltpu.VMEM((rows, cols, bands), bf16),
             pltpu.VMEM((bands, bands), f32),

time: 37.6 us -> 37.7 us (level)
  no operation moved by 1% of the time
where the time goes in v3:
time: 37.7 us; the launch traced here: 37.3 us
  starting transfers between devices  20.7 us (55%)
  Pallas kernels  10 us (27%)
  waiting for transfers between devices  5.77 us (15%)
  between operations  0.77 us (2%)
    all_to_all x2, starting transfers between devices, exchange(): return lax.all_to_all(pieces, axes, split_axis=0, concat_axis=0)  11.4 us
    all_to_all x2, waiting for transfers between devices, exchange(): return lax.all_to_all(pieces, axes, split_axis=0, concat_axis=0)  5.76 us
    pallas_call x1, Pallas kernels, body(): pl.pallas_call(functools.partial(main_kernel, depth, n_rows, n_cols), in_...  4.65 us
    ppermute x1, starting transfers between devices, neighbours(): before = lax.ppermute(tail, axis, [(i, i + 1) for i in range(count - 1)])  4.55 us
    pallas_call x1, Pallas kernels, body(): pl.pallas_call(gram_kernel, in_specs=[pl.BlockSpec(memory_space=pl.ANY)],...  2.36 us
    pallas_call x1, Pallas kernels, body(): pl.pallas_call(functools.partial(subspace_kernel, inv_count), in_specs=[v...  2.27 us
    ppermute x1, starting transfers between devices, body(): lax.ppermute(down, 'narrow', [(i, i + 1) for i in range(n_rows - 1)])  2.16 us
    ppermute x1, starting transfers between devices, neighbours(): after = lax.ppermute(head, axis, [(i + 1, i) for i in range(count - 1)])  1.29 us
  transfers between devices with their start and end apart: 6, of which 2 were waited for; matrix products, arithmetic and copies ran while one was open for 0% of the time, Pallas kernels for 8%

profile of v3, /device:TPU:0, one launch (start us, length us, event | category | flops | bytes accessed | tf_op | source)
XLA Modules:
  0.0 37.3 jit_solution(18017956096677726852)
XLA Ops:
  0.6 0.0 copy-start
  0.6 2.4 %shard_map.41 = f32[224,128]{1,0:T(8,128)} custom-call(bf16[32,48,224]{2,1,0:T(8,128)(2,1)} %mid_ref), custom_call_target="tpu_custom_call" | custom-call | tf_op jit(solution)/shard_map/pallas_call | solution.py:382
  3.0 7.3 %all-to-all-start = ((f32[32,1,896]{2,1,0:T(1,128)}), f32[32,1,896]{2,1,0:T(1,128)S(1)}, u32[]{:S(2)}, u32[]{:S(2)}) async-start(f32[32,1,896]{2,1,0:T(1,128)} %bitcast.6), calls=%async_computation | async-start | bytes 229376 | tf_op jit(solution)/shard_map/all_to_all | solution.py:369
  10.3 0.0 copy-done
  10.3 0.1 fusion.1
  10.4 1.3 %collective-permute-start.1 = (bf16[32,3,224]{2,1,0:T(4,128)(2,1)S(1)}, bf16[32,3,224]{2,1,0:T(4,128)(2,1)S(1)}, u32[]{:S(2)}, u32[]{:S(2)}) collective-permute-start(bf16[32,3,224]{2,1,0:T(4,128)(2,1)S(1)} %get-tuple-element.14), channel_id=1, source_target_pairs={{4,0},{8,4},{12,8},{16,12},{20,16},{24,20},{28,24},{5,1},{9,5},{13... | collective-permute-start | bytes 129032 | tf_op jit(solution)/shard_map/ppermute | solution.py:364
  11.7 4.5 %collective-permute-start = (bf16[32,3,224]{2,1,0:T(4,128)(2,1)S(1)}, bf16[32,3,224]{2,1,0:T(4,128)(2,1)S(1)}, u32[]{:S(2)}, u32[]{:S(2)}) collective-permute-start(bf16[32,3,224]{2,1,0:T(4,128)(2,1)S(1)} %get-tuple-element.15), channel_id=1, source_target_pairs={{0,4},{4,8},{8,12},{12,16},{16,20},{20,24},{24,28},{1,5},{5,9},{9,... | collective-permute-start | bytes 129032 | tf_op jit(solution)/shard_map/ppermute | solution.py:363
  16.3 1.7 %all-to-all-done = f32[32,1,896]{2,1,0:T(1,128)S(1)} async-done(((f32[32,1,896]{2,1,0:T(1,128)}), f32[32,1,896]{2,1,0:T(1,128)S(1)}, u32[]{:S(2)}, u32[]{:S(2)}) %all-to-all-start) | async-done | bytes 114720 | tf_op jit(solution)/shard_map/all_to_all | solution.py:369
  18.0 0.7 %shard_map.42 = f32[224,128]{1,0:T(8,128)} custom-call(f32[224,128]{1,0:T(8,128)S(1)} %bitcast.4), custom_call_target="tpu_custom_call" | custom-call | tf_op jit(solution)/shard_map/pallas_call | solution.py:398
  18.7 4.1 %all-to-all-start.1 = ((f32[32,1,896]{2,1,0:T(1,128)}), f32[32,1,896]{2,1,0:T(1,128)S(1)}, u32[]{:S(2)}, u32[]{:S(2)}) async-start(f32[32,1,896]{2,1,0:T(1,128)} %bitcast.2), calls=%async_computation.1 | async-start | bytes 229376 | tf_op jit(solution)/shard_map/all_to_all | solution.py:369
  22.7 0.0 collective-permute-done.1.right_ref
  22.8 0.0 collective-permute-done.left_ref
  22.8 0.0 copy-start.1
  22.8 0.1 shard_map.44
  22.9 2.2 %collective-permute-start.2 = (bf16[3,56,224]{2,1,0:T(8,128)(2,1)S(1)}, bf16[3,56,224]{2,1,0:T(8,128)(2,1)S(1)}, u32[]{:S(2)}, u32[]{:S(2)}) collective-permute-start(bf16[3,56,224]{2,1,0:T(8,128)(2,1)S(1)} %get-tuple-element.9), channel_id=1, source_target_pairs={{0,1},{1,2},{2,3},{4,5},{5,6},{6,7},{8,9},{9,10},{10,11},{12,13},{... | collective-permute-start | bytes 225800 | tf_op jit(solution)/shard_map/ppermute | solution.py:421
  25.0 1.3 %collective-permute-start.3 = (bf16[3,56,224]{2,1,0:T(8,128)(2,1)S(1)}, bf16[3,56,224]{2,1,0:T(8,128)(2,1)S(1)}, u32[]{:S(2)}, u32[]{:S(2)}) collective-permute-start(bf16[3,56,224]{2,1,0:T(8,128)(2,1)S(1)} %get-tuple-element.10), channel_id=1, source_target_pairs={{1,0},{2,1},{3,2},{5,4},{6,5},{7,6},{9,8},{10,9},{11,10},{13,12},{... | collective-permute-start | bytes 225800 | tf_op jit(solution)/shard_map/ppermute | solution.py:422
  26.3 4.1 %all-to-all-done.1 = f32[32,1,896]{2,1,0:T(1,128)S(1)} async-done(((f32[32,1,896]{2,1,0:T(1,128)}), f32[32,1,896]{2,1,0:T(1,128)S(1)}, u32[]{:S(2)}, u32[]{:S(2)}) %all-to-all-start.1) | async-done | bytes 114720 | tf_op jit(solution)/shard_map/all_to_all | solution.py:369
  30.4 0.0 copy-done.1
  30.4 2.3 %shard_map.43.basis_ref = f32[16,256]{1,0:T(8,128)S(1)} custom-call(f32[224,128]{1,0:T(8,128)S(1)} %bitcast.5, f32[16,256]{1,0:T(8,128)S(1)} %copy-done.1), custom_call_target="tpu_custom_call" | custom-call | flops 4294967296 | bytes 262144 | tf_op jit(solution)/shard_map/pallas_call | solution.py:425
  32.7 0.0 collective-permute-done.2.above_ref
  32.7 0.0 collective-permute-done.3.below_ref
  32.7 4.6 %shard_map.45 = (bf16[32,48,224]{2,1,0:T(8,128)(2,1)}, f32[224,224]{1,0:T(8,128)}) custom-call(f32[16,256]{1,0:T(8,128)S(1)} %shard_map.43.basis_ref, bf16[32,48,224]{2,1,0:T(8,128)(2,1)S(1)} %copy-done, bf16[3,56,224]{2,1,0:T(8,128)(2,1)S(1)} %collective-permute-done.2.above_ref, bf16[3,56,224]{2,1,0:T(8,128)(2,1)S(1)} %collective-permute-done.3.below_ref, ...), custom_call_target="tpu_custom_call" | custom-call | tf_op jit(solution)/shard_map/pallas_call | solution.py:434
  (1 shorter events, 0.0 us)
Async XLA Ops:
  0.6 9.7 %copy-start = (bf16[32,48,224]{2,1,0:T(8,128)(2,1)S(1)}, bf16[32,48,224]{2,1,0:T(8,128)(2,1)}, u32[]{:S(2)}) copy-start(bf16[32,48,224]{2,1,0:T(8,128)(2,1)} %mid_ref) | copy-start | bytes 2064388
  3.0 15.0 %all-to-all-start = ((f32[32,1,896]{2,1,0:T(1,128)}), f32[32,1,896]{2,1,0:T(1,128)S(1)}, u32[]{:S(2)}, u32[]{:S(2)}) async-start(f32[32,1,896]{2,1,0:T(1,128)} %bitcast.6), calls=%async_computation | async-start | bytes 229376 | tf_op jit(solution)/shard_map/all_to_all | solution.py:369
  10.4 12.4 %collective-permute-start.1 = (bf16[32,3,224]{2,1,0:T(4,128)(2,1)S(1)}, bf16[32,3,224]{2,1,0:T(4,128)(2,1)S(1)}, u32[]{:S(2)}, u32[]{:S(2)}) collective-permute-start(bf16[32,3,224]{2,1,0:T(4,128)(2,1)S(1)} %get-tuple-element.14), channel_id=1, source_target_pairs={{4,0},{8,4},{12,8},{16,12},{20,16},{24,20},{28,24},{5,1},{9,5},{13... | collective-permute-start | bytes 129032 | tf_op jit(solution)/shard_map/ppermute | solution.py:364
  11.7 11.1 %collective-permute-start = (bf16[32,3,224]{2,1,0:T(4,128)(2,1)S(1)}, bf16[32,3,224]{2,1,0:T(4,128)(2,1)S(1)}, u32[]{:S(2)}, u32[]{:S(2)}) collective-permute-start(bf16[32,3,224]{2,1,0:T(4,128)(2,1)S(1)} %get-tuple-element.15), channel_id=1, source_target_pairs={{0,4},{4,8},{8,12},{12,16},{16,20},{20,24},{24,28},{1,5},{5,9},{9,... | collective-permute-start | bytes 129032 | tf_op jit(solution)/shard_map/ppermute | solution.py:363
  18.7 11.7 %all-to-all-start.1 = ((f32[32,1,896]{2,1,0:T(1,128)}), f32[32,1,896]{2,1,0:T(1,128)S(1)}, u32[]{:S(2)}, u32[]{:S(2)}) async-start(f32[32,1,896]{2,1,0:T(1,128)} %bitcast.2), calls=%async_computation.1 | async-start | bytes 229376 | tf_op jit(solution)/shard_map/all_to_all | solution.py:369
  22.8 7.6 %copy-start.1 = (f32[16,256]{1,0:T(8,128)S(1)}, f32[16,256]{1,0:T(8,128)}, u32[]{:S(2)}) copy-start(f32[16,256]{1,0:T(8,128)} %constant.2.clone.start_ref) | copy-start | bytes 49156
  22.9 9.8 %collective-permute-start.2 = (bf16[3,56,224]{2,1,0:T(8,128)(2,1)S(1)}, bf16[3,56,224]{2,1,0:T(8,128)(2,1)S(1)}, u32[]{:S(2)}, u32[]{:S(2)}) collective-permute-start(bf16[3,56,224]{2,1,0:T(8,128)(2,1)S(1)} %get-tuple-element.9), channel_id=1, source_target_pairs={{0,1},{1,2},{2,3},{4,5},{5,6},{6,7},{8,9},{9,10},{10,11},{12,13},{... | collective-permute-start | bytes 225800 | tf_op jit(solution)/shard_map/ppermute | solution.py:421
  25.0 7.7 %collective-permute-start.3 = (bf16[3,56,224]{2,1,0:T(8,128)(2,1)S(1)}, bf16[3,56,224]{2,1,0:T(8,128)(2,1)S(1)}, u32[]{:S(2)}, u32[]{:S(2)}) collective-permute-start(bf16[3,56,224]{2,1,0:T(8,128)(2,1)S(1)} %get-tuple-element.10), channel_id=1, source_target_pairs={{1,0},{2,1},{3,2},{5,4},{6,5},{7,6},{9,8},{10,9},{11,10},{13,12},{... | collective-permute-start | bytes 225800 | tf_op jit(solution)/shard_map/ppermute | solution.py:422

commit v4 on v1

--- a/solution.py
+++ b/solution.py
@@ -198,15 +198,10 @@
         tn,
         preferred_element_type=f32,
     )
-    mixed = mixed * 4.0
-    mixed_high = mixed.astype(bf16)
-    mixed_low = (mixed - mixed_high.astype(f32)).astype(bf16)
-    mixed_both = jnp.concatenate([mixed_high, mixed_low], axis=0)
+    mixed = (mixed[:bands] * 4.0).astype(bf16)
 
     def fitted(flat):
-        padded = jnp.concatenate([flat, jnp.zeros((flat.shape[0], LANES - bands), bf16)], axis=1)
-        both = jnp.concatenate([padded, padded], axis=1)
-        return jnp.dot(both, mixed_both, preferred_element_type=f32)
+        return jnp.dot(flat, mixed, preferred_element_type=f32)
 
     def project():
         right = jnp.concatenate([high, high, high, mid, mid, low], axis=0)

time: 37.6 us -> 37.5 us (level)
  no operation moved by 1% of the time
where the time goes in v4:
time: 37.5 us; the launch traced here: 37.2 us
  starting transfers between devices  20.7 us (55%)
  Pallas kernels  9.86 us (26%)
  waiting for transfers between devices  5.77 us (15%)
  between operations  0.77 us (2%)
    all_to_all x2, starting transfers between devices, exchange(): return lax.all_to_all(pieces, axes, split_axis=0, concat_axis=0)  11.4 us
    all_to_all x2, waiting for transfers between devices, exchange(): return lax.all_to_all(pieces, axes, split_axis=0, concat_axis=0)  5.76 us
    ppermute x1, starting transfers between devices, neighbours(): before = lax.ppermute(tail, axis, [(i, i + 1) for i in range(count - 1)])  4.55 us
    pallas_call x1, Pallas kernels, body(): pl.pallas_call(functools.partial(main_kernel, depth, n_rows, n_cols), in_...  4.47 us
    pallas_call x1, Pallas kernels, body(): pl.pallas_call(gram_kernel, in_specs=[pl.BlockSpec(memory_space=pl.ANY)],...  2.36 us
    pallas_call x1, Pallas kernels, body(): pl.pallas_call(functools.partial(subspace_kernel, inv_count), in_specs=[v...  2.27 us
    ppermute x1, starting transfers between devices, body(): lax.ppermute(down, 'narrow', [(i, i + 1) for i in range(n_rows - 1)])  2.16 us
    ppermute x1, starting transfers between devices, neighbours(): after = lax.ppermute(head, axis, [(i + 1, i) for i in range(count - 1)])  1.29 us
  transfers between devices with their start and end apart: 6, of which 2 were waited for; matrix products, arithmetic and copies ran while one was open for 0% of the time, Pallas kernels for 8%

profile of v4, /device:TPU:0, one launch (start us, length us, event | category | flops | bytes accessed | tf_op | source)
XLA Modules:
  0.0 37.2 jit_solution(5890806715648348021)
XLA Ops:
  0.6 0.0 copy-start
  0.6 2.4 %shard_map.41 = f32[224,128]{1,0:T(8,128)} custom-call(bf16[32,48,224]{2,1,0:T(8,128)(2,1)} %mid_ref), custom_call_target="tpu_custom_call" | custom-call | tf_op jit(solution)/shard_map/pallas_call | solution.py:375
  3.0 7.3 %all-to-all-start = ((f32[32,1,896]{2,1,0:T(1,128)}), f32[32,1,896]{2,1,0:T(1,128)S(1)}, u32[]{:S(2)}, u32[]{:S(2)}) async-start(f32[32,1,896]{2,1,0:T(1,128)} %bitcast.6), calls=%async_computation | async-start | bytes 229376 | tf_op jit(solution)/shard_map/all_to_all | solution.py:362
  10.3 0.0 copy-done
  10.3 0.1 fusion.1
  10.4 1.3 %collective-permute-start.1 = (bf16[32,3,224]{2,1,0:T(4,128)(2,1)S(1)}, bf16[32,3,224]{2,1,0:T(4,128)(2,1)S(1)}, u32[]{:S(2)}, u32[]{:S(2)}) collective-permute-start(bf16[32,3,224]{2,1,0:T(4,128)(2,1)S(1)} %get-tuple-element.14), channel_id=1, source_target_pairs={{4,0},{8,4},{12,8},{16,12},{20,16},{24,20},{28,24},{5,1},{9,5},{13... | collective-permute-start | bytes 129032 | tf_op jit(solution)/shard_map/ppermute | solution.py:357
  11.7 4.5 %collective-permute-start = (bf16[32,3,224]{2,1,0:T(4,128)(2,1)S(1)}, bf16[32,3,224]{2,1,0:T(4,128)(2,1)S(1)}, u32[]{:S(2)}, u32[]{:S(2)}) collective-permute-start(bf16[32,3,224]{2,1,0:T(4,128)(2,1)S(1)} %get-tuple-element.15), channel_id=1, source_target_pairs={{0,4},{4,8},{8,12},{12,16},{16,20},{20,24},{24,28},{1,5},{5,9},{9,... | collective-permute-start | bytes 129032 | tf_op jit(solution)/shard_map/ppermute | solution.py:356
  16.3 1.7 %all-to-all-done = f32[32,1,896]{2,1,0:T(1,128)S(1)} async-done(((f32[32,1,896]{2,1,0:T(1,128)}), f32[32,1,896]{2,1,0:T(1,128)S(1)}, u32[]{:S(2)}, u32[]{:S(2)}) %all-to-all-start) | async-done | bytes 114720 | tf_op jit(solution)/shard_map/all_to_all | solution.py:362
  18.0 0.7 %shard_map.42 = f32[224,128]{1,0:T(8,128)} custom-call(f32[224,128]{1,0:T(8,128)S(1)} %bitcast.4), custom_call_target="tpu_custom_call" | custom-call | tf_op jit(solution)/shard_map/pallas_call | solution.py:391
  18.7 4.1 %all-to-all-start.1 = ((f32[32,1,896]{2,1,0:T(1,128)}), f32[32,1,896]{2,1,0:T(1,128)S(1)}, u32[]{:S(2)}, u32[]{:S(2)}) async-start(f32[32,1,896]{2,1,0:T(1,128)} %bitcast.2), calls=%async_computation.1 | async-start | bytes 229376 | tf_op jit(solution)/shard_map/all_to_all | solution.py:362
  22.7 0.0 collective-permute-done.1.right_ref
  22.8 0.0 collective-permute-done.left_ref
  22.8 0.0 copy-start.1
  22.8 0.1 shard_map.44
  22.9 2.2 %collective-permute-start.2 = (bf16[3,56,224]{2,1,0:T(8,128)(2,1)S(1)}, bf16[3,56,224]{2,1,0:T(8,128)(2,1)S(1)}, u32[]{:S(2)}, u32[]{:S(2)}) collective-permute-start(bf16[3,56,224]{2,1,0:T(8,128)(2,1)S(1)} %get-tuple-element.9), channel_id=1, source_target_pairs={{0,1},{1,2},{2,3},{4,5},{5,6},{6,7},{8,9},{9,10},{10,11},{12,13},{... | collective-permute-start | bytes 225800 | tf_op jit(solution)/shard_map/ppermute | solution.py:414
  25.0 1.3 %collective-permute-start.3 = (bf16[3,56,224]{2,1,0:T(8,128)(2,1)S(1)}, bf16[3,56,224]{2,1,0:T(8,128)(2,1)S(1)}, u32[]{:S(2)}, u32[]{:S(2)}) collective-permute-start(bf16[3,56,224]{2,1,0:T(8,128)(2,1)S(1)} %get-tuple-element.10), channel_id=1, source_target_pairs={{1,0},{2,1},{3,2},{5,4},{6,5},{7,6},{9,8},{10,9},{11,10},{13,12},{... | collective-permute-start | bytes 225800 | tf_op jit(solution)/shard_map/ppermute | solution.py:415
  26.3 4.1 %all-to-all-done.1 = f32[32,1,896]{2,1,0:T(1,128)S(1)} async-done(((f32[32,1,896]{2,1,0:T(1,128)}), f32[32,1,896]{2,1,0:T(1,128)S(1)}, u32[]{:S(2)}, u32[]{:S(2)}) %all-to-all-start.1) | async-done | bytes 114720 | tf_op jit(solution)/shard_map/all_to_all | solution.py:362
  30.4 0.0 copy-done.1
  30.4 2.3 %shard_map.43.basis_ref = f32[16,256]{1,0:T(8,128)S(1)} custom-call(f32[224,128]{1,0:T(8,128)S(1)} %bitcast.5, f32[16,256]{1,0:T(8,128)S(1)} %copy-done.1), custom_call_target="tpu_custom_call" | custom-call | flops 4294967296 | bytes 262144 | tf_op jit(solution)/shard_map/pallas_call | solution.py:418
  32.7 0.0 collective-permute-done.2.above_ref
  32.7 0.0 collective-permute-done.3.below_ref
  32.7 4.5 %shard_map.45 = (bf16[32,48,224]{2,1,0:T(8,128)(2,1)}, f32[224,224]{1,0:T(8,128)}) custom-call(f32[16,256]{1,0:T(8,128)S(1)} %shard_map.43.basis_ref, bf16[32,48,224]{2,1,0:T(8,128)(2,1)S(1)} %copy-done, bf16[3,56,224]{2,1,0:T(8,128)(2,1)S(1)} %collective-permute-done.2.above_ref, bf16[3,56,224]{2,1,0:T(8,128)(2,1)S(1)} %collective-permute-done.3.below_ref, ...), custom_call_target="tpu_custom_call" | custom-call | tf_op jit(solution)/shard_map/pallas_call | solution.py:427
  (1 shorter events, 0.0 us)
Async XLA Ops:
  0.6 9.7 %copy-start = (bf16[32,48,224]{2,1,0:T(8,128)(2,1)S(1)}, bf16[32,48,224]{2,1,0:T(8,128)(2,1)}, u32[]{:S(2)}) copy-start(bf16[32,48,224]{2,1,0:T(8,128)(2,1)} %mid_ref) | copy-start | bytes 2064388
  3.0 15.0 %all-to-all-start = ((f32[32,1,896]{2,1,0:T(1,128)}), f32[32,1,896]{2,1,0:T(1,128)S(1)}, u32[]{:S(2)}, u32[]{:S(2)}) async-start(f32[32,1,896]{2,1,0:T(1,128)} %bitcast.6), calls=%async_computation | async-start | bytes 229376 | tf_op jit(solution)/shard_map/all_to_all | solution.py:362
  10.4 12.4 %collective-permute-start.1 = (bf16[32,3,224]{2,1,0:T(4,128)(2,1)S(1)}, bf16[32,3,224]{2,1,0:T(4,128)(2,1)S(1)}, u32[]{:S(2)}, u32[]{:S(2)}) collective-permute-start(bf16[32,3,224]{2,1,0:T(4,128)(2,1)S(1)} %get-tuple-element.14), channel_id=1, source_target_pairs={{4,0},{8,4},{12,8},{16,12},{20,16},{24,20},{28,24},{5,1},{9,5},{13... | collective-permute-start | bytes 129032 | tf_op jit(solution)/shard_map/ppermute | solution.py:357
  11.7 11.1 %collective-permute-start = (bf16[32,3,224]{2,1,0:T(4,128)(2,1)S(1)}, bf16[32,3,224]{2,1,0:T(4,128)(2,1)S(1)}, u32[]{:S(2)}, u32[]{:S(2)}) collective-permute-start(bf16[32,3,224]{2,1,0:T(4,128)(2,1)S(1)} %get-tuple-element.15), channel_id=1, source_target_pairs={{0,4},{4,8},{8,12},{12,16},{16,20},{20,24},{24,28},{1,5},{5,9},{9,... | collective-permute-start | bytes 129032 | tf_op jit(solution)/shard_map/ppermute | solution.py:356
  18.7 11.7 %all-to-all-start.1 = ((f32[32,1,896]{2,1,0:T(1,128)}), f32[32,1,896]{2,1,0:T(1,128)S(1)}, u32[]{:S(2)}, u32[]{:S(2)}) async-start(f32[32,1,896]{2,1,0:T(1,128)} %bitcast.2), calls=%async_computation.1 | async-start | bytes 229376 | tf_op jit(solution)/shard_map/all_to_all | solution.py:362
  22.8 7.6 %copy-start.1 = (f32[16,256]{1,0:T(8,128)S(1)}, f32[16,256]{1,0:T(8,128)}, u32[]{:S(2)}) copy-start(f32[16,256]{1,0:T(8,128)} %constant.2.clone.start_ref) | copy-start | bytes 49156
  22.9 9.8 %collective-permute-start.2 = (bf16[3,56,224]{2,1,0:T(8,128)(2,1)S(1)}, bf16[3,56,224]{2,1,0:T(8,128)(2,1)S(1)}, u32[]{:S(2)}, u32[]{:S(2)}) collective-permute-start(bf16[3,56,224]{2,1,0:T(8,128)(2,1)S(1)} %get-tuple-element.9), channel_id=1, source_target_pairs={{0,1},{1,2},{2,3},{4,5},{5,6},{6,7},{8,9},{9,10},{10,11},{12,13},{... | collective-permute-start | bytes 225800 | tf_op jit(solution)/shard_map/ppermute | solution.py:414
  25.0 7.7 %collective-permute-start.3 = (bf16[3,56,224]{2,1,0:T(8,128)(2,1)S(1)}, bf16[3,56,224]{2,1,0:T(8,128)(2,1)S(1)}, u32[]{:S(2)}, u32[]{:S(2)}) collective-permute-start(bf16[3,56,224]{2,1,0:T(8,128)(2,1)S(1)} %get-tuple-element.10), channel_id=1, source_target_pairs={{1,0},{2,1},{3,2},{5,4},{6,5},{7,6},{9,8},{10,9},{11,10},{13,12},{... | collective-permute-start | bytes 225800 | tf_op jit(solution)/shard_map/ppermute | solution.py:415

commit v5 on v1

--- a/solution.py
+++ b/solution.py
@@ -31,25 +31,13 @@
     return lax.broadcasted_iota(jnp.int32, shape, 0), lax.broadcasted_iota(jnp.int32, shape, 1)
 
 
-def gram_kernel(cube_ref, packed_ref, block, full, sems):
+def gram_kernel(cube_ref, packed_ref, full):
     rows, cols, bands = cube_ref.shape
-    pieces = sems.shape[0]
-    high = rows // pieces
-
-    def copy(n):
-        part = pl.ds(n * high, high)
-        return pltpu.make_async_copy(cube_ref.at[part], block.at[part], sems.at[n])
-
-    for n in range(pieces):
-        copy(n).start()
+    flat = cube_ref[...].reshape(rows * cols, bands)
     full[HALF:, HALF:] = jnp.zeros((LANES - HALF, LANES - HALF), f32)
-    total = None
-    for n in range(pieces):
-        copy(n).wait()
-        flat = block[n * high : (n + 1) * high].reshape(high * cols, bands)
-        term = lax.dot_general(flat, flat, (((0,), (0,)), ((), ())), preferred_element_type=f32)
-        total = term if total is None else total + term
-    full[0:bands, 0:bands] = total
+    full[0:bands, 0:bands] = lax.dot_general(
+        flat, flat, (((0,), (0,)), ((), ())), preferred_element_type=f32
+    )
     i, j = iotas((HALF, HALF))
     first = full[0:HALF, 0:HALF]
     second = pltpu.roll(full[HALF:LANES, HALF:LANES], 1, 1)
@@ -376,21 +364,17 @@
     axes = ("narrow", "wide")
 
     tall_packed = -(-bands // count) * count
-    pieces = 2 if rows % 2 == 0 else 1
+    vmem = pl.BlockSpec(memory_space=pltpu.VMEM)
     packed = pl.pallas_call(
         gram_kernel,
-        in_specs=[pl.BlockSpec(memory_space=pl.ANY)],
+        in_specs=[vmem],
+        out_specs=vmem,
         out_shape=jax.ShapeDtypeStruct((tall_packed, HALF), f32),
-        scratch_shapes=[
-            pltpu.VMEM(cube.shape, cube.dtype),
-            pltpu.VMEM((LANES, LANES), f32),
-            pltpu.SemaphoreType.DMA((pieces,)),
-        ],
-        compiler_params=pltpu.CompilerParams(vmem_limit_bytes=62 * 2**20),
+        scratch_shapes=[pltpu.VMEM((LANES, LANES), f32)],
+        compiler_params=pltpu.CompilerParams(vmem_limit_bytes=32 * 2**20),
     )(cube)
     packed, cube = lax.optimization_barrier((packed, cube))
     left, right = neighbours(cube, "wide", 1, depth)
-    vmem = pl.BlockSpec(memory_space=pltpu.VMEM)
     pieces_shape = (count, 1, tall_packed // count * HALF)
     part = exchange(packed.reshape(pieces_shape), axes).reshape(tall_packed, HALF)
     share = pl.pallas_call(

time: 37.6 us -> 37.6 us (level)
  Pallas kernels: 9.99 us -> 8.79 us
  local copies, waits for them, and re-layouts: 0.08 us -> 1.2 us
    pallas_call x1, Pallas kernels: 2.36 us -> 1.16 us  [body(): pl.pallas_call(gram_kernel, in_specs=[vmem], out_specs=vmem, out_shape=ja...]
    unnamed x4 -> x6, local copies, waits for them, and re-layouts: 0.01 us -> 1.14 us
where the time goes in v5:
time: 37.6 us; the launch traced here: 37.2 us
  starting transfers between devices  20.7 us (55%)
  Pallas kernels  8.79 us (23%)
  waiting for transfers between devices  5.77 us (15%)
  local copies, waits for them, and re-layouts  1.2 us (3%)
  between operations  0.76 us (2%)
    all_to_all x2, starting transfers between devices, exchange(): return lax.all_to_all(pieces, axes, split_axis=0, concat_axis=0)  11.4 us
    all_to_all x2, waiting for transfers between devices, exchange(): return lax.all_to_all(pieces, axes, split_axis=0, concat_axis=0)  5.76 us
    pallas_call x1, Pallas kernels, body(): pl.pallas_call(functools.partial(main_kernel, depth, n_rows, n_cols), in_...  4.59 us
    ppermute x1, starting transfers between devices, neighbours(): before = lax.ppermute(tail, axis, [(i, i + 1) for i in range(count - 1)])  4.55 us
    pallas_call x1, Pallas kernels, body(): pl.pallas_call(functools.partial(subspace_kernel, inv_count), in_specs=[v...  2.27 us
    ppermute x1, starting transfers between devices, body(): lax.ppermute(down, 'narrow', [(i, i + 1) for i in range(n_rows - 1)])  2.16 us
    ppermute x1, starting transfers between devices, neighbours(): after = lax.ppermute(head, axis, [(i + 1, i) for i in range(count - 1)])  1.29 us
    ppermute x1, starting transfers between devices, body(): below = lax.ppermute(up, 'narrow', [(i + 1, i) for i in range(n_rows - 1)])  1.29 us
  transfers between devices with their start and end apart: 6, of which 2 were waited for; matrix products, arithmetic and copies ran while one was open for 0% of the time, Pallas kernels for 8%

profile of v5, /device:TPU:0, one launch (start us, length us, event | category | flops | bytes accessed | tf_op | source)
XLA Modules:
  0.0 37.2 jit_solution(9858974431219827353)
XLA Ops:
  0.6 0.0 copy-start
  0.6 1.1 %copy-done = bf16[32,48,224]{2,1,0:T(8,128)(2,1)S(1)} copy-done((bf16[32,48,224]{2,1,0:T(8,128)(2,1)S(1)}, bf16[32,48,224]{2,1,0:T(8,128)(2,1)}, u32[]{:S(2)}) %copy-start) | copy-done | bytes 688152
  1.8 0.0 copy-start.1
  1.8 1.2 %shard_map.41 = f32[224,128]{1,0:T(8,128)} custom-call(bf16[32,48,224]{2,1,0:T(8,128)(2,1)S(1)} %copy-done), custom_call_target="tpu_custom_call" | custom-call | tf_op jit(solution)/shard_map/pallas_call | solution.py:368
  2.9 7.3 %all-to-all-start = ((f32[32,1,896]{2,1,0:T(1,128)}), f32[32,1,896]{2,1,0:T(1,128)S(1)}, u32[]{:S(2)}, u32[]{:S(2)}) async-start(f32[32,1,896]{2,1,0:T(1,128)} %bitcast), calls=%async_computation | async-start | bytes 229376 | tf_op jit(solution)/shard_map/all_to_all | solution.py:355
  10.2 0.0 copy-done.1
  10.2 0.1 fusion.1
  10.3 1.3 %collective-permute-start.1 = (bf16[32,3,224]{2,1,0:T(4,128)(2,1)S(1)}, bf16[32,3,224]{2,1,0:T(4,128)(2,1)S(1)}, u32[]{:S(2)}, u32[]{:S(2)}) collective-permute-start(bf16[32,3,224]{2,1,0:T(4,128)(2,1)S(1)} %get-tuple-element.14), channel_id=1, source_target_pairs={{4,0},{8,4},{12,8},{16,12},{20,16},{24,20},{28,24},{5,1},{9,5},{13... | collective-permute-start | bytes 129032 | tf_op jit(solution)/shard_map/ppermute | solution.py:350
  11.6 4.5 %collective-permute-start = (bf16[32,3,224]{2,1,0:T(4,128)(2,1)S(1)}, bf16[32,3,224]{2,1,0:T(4,128)(2,1)S(1)}, u32[]{:S(2)}, u32[]{:S(2)}) collective-permute-start(bf16[32,3,224]{2,1,0:T(4,128)(2,1)S(1)} %get-tuple-element.15), channel_id=1, source_target_pairs={{0,4},{4,8},{8,12},{12,16},{16,20},{20,24},{24,28},{1,5},{5,9},{9,... | collective-permute-start | bytes 129032 | tf_op jit(solution)/shard_map/ppermute | solution.py:349
  16.2 1.7 %all-to-all-done = f32[32,1,896]{2,1,0:T(1,128)S(1)} async-done(((f32[32,1,896]{2,1,0:T(1,128)}), f32[32,1,896]{2,1,0:T(1,128)S(1)}, u32[]{:S(2)}, u32[]{:S(2)}) %all-to-all-start) | async-done | bytes 114720 | tf_op jit(solution)/shard_map/all_to_all | solution.py:355
  17.9 0.7 %shard_map.42 = f32[224,128]{1,0:T(8,128)} custom-call(f32[224,128]{1,0:T(8,128)S(1)} %bitcast.4), custom_call_target="tpu_custom_call" | custom-call | tf_op jit(solution)/shard_map/pallas_call | solution.py:380
  18.6 4.1 %all-to-all-start.1 = ((f32[32,1,896]{2,1,0:T(1,128)}), f32[32,1,896]{2,1,0:T(1,128)S(1)}, u32[]{:S(2)}, u32[]{:S(2)}) async-start(f32[32,1,896]{2,1,0:T(1,128)} %bitcast.2), calls=%async_computation.1 | async-start | bytes 229376 | tf_op jit(solution)/shard_map/all_to_all | solution.py:355
  22.7 0.0 collective-permute-done.1.right_ref
  22.7 0.0 collective-permute-done.left_ref
  22.7 0.0 copy-start.2
  22.7 0.1 shard_map.44
  22.8 2.2 %collective-permute-start.2 = (bf16[3,56,224]{2,1,0:T(8,128)(2,1)S(1)}, bf16[3,56,224]{2,1,0:T(8,128)(2,1)S(1)}, u32[]{:S(2)}, u32[]{:S(2)}) collective-permute-start(bf16[3,56,224]{2,1,0:T(8,128)(2,1)S(1)} %get-tuple-element.9), channel_id=1, source_target_pairs={{0,1},{1,2},{2,3},{4,5},{5,6},{6,7},{8,9},{9,10},{10,11},{12,13},{... | collective-permute-start | bytes 225800 | tf_op jit(solution)/shard_map/ppermute | solution.py:403
  24.9 1.3 %collective-permute-start.3 = (bf16[3,56,224]{2,1,0:T(8,128)(2,1)S(1)}, bf16[3,56,224]{2,1,0:T(8,128)(2,1)S(1)}, u32[]{:S(2)}, u32[]{:S(2)}) collective-permute-start(bf16[3,56,224]{2,1,0:T(8,128)(2,1)S(1)} %get-tuple-element.10), channel_id=1, source_target_pairs={{1,0},{2,1},{3,2},{5,4},{6,5},{7,6},{9,8},{10,9},{11,10},{13,12},{... | collective-permute-start | bytes 225800 | tf_op jit(solution)/shard_map/ppermute | solution.py:404
  26.2 4.1 %all-to-all-done.1 = f32[32,1,896]{2,1,0:T(1,128)S(1)} async-done(((f32[32,1,896]{2,1,0:T(1,128)}), f32[32,1,896]{2,1,0:T(1,128)S(1)}, u32[]{:S(2)}, u32[]{:S(2)}) %all-to-all-start.1) | async-done | bytes 114720 | tf_op jit(solution)/shard_map/all_to_all | solution.py:355
  30.3 0.0 copy-done.2
  30.3 2.3 %shard_map.43.basis_ref = f32[16,256]{1,0:T(8,128)S(1)} custom-call(f32[224,128]{1,0:T(8,128)S(1)} %bitcast.5, f32[16,256]{1,0:T(8,128)S(1)} %copy-done.2), custom_call_target="tpu_custom_call" | custom-call | flops 4294967296 | bytes 262144 | tf_op jit(solution)/shard_map/pallas_call | solution.py:407
  32.6 0.0 collective-permute-done.2.above_ref
  32.6 0.0 collective-permute-done.3.below_ref
  32.6 4.6 %shard_map.45 = (bf16[32,48,224]{2,1,0:T(8,128)(2,1)}, f32[224,224]{1,0:T(8,128)}) custom-call(f32[16,256]{1,0:T(8,128)S(1)} %shard_map.43.basis_ref, bf16[32,48,224]{2,1,0:T(8,128)(2,1)S(1)} %copy-done.1, bf16[3,56,224]{2,1,0:T(8,128)(2,1)S(1)} %collective-permute-done.2.above_ref, bf16[3,56,224]{2,1,0:T(8,128)(2,1)S(1)} %collective-permute-done.3.below_ref, ...), custom_call_target="tpu_custom_call" | custom-call | tf_op jit(solution)/shard_map/pallas_call | solution.py:416
  (1 shorter events, 0.0 us)
Async XLA Ops:
  0.6 1.1 %copy-start = (bf16[32,48,224]{2,1,0:T(8,128)(2,1)S(1)}, bf16[32,48,224]{2,1,0:T(8,128)(2,1)}, u32[]{:S(2)}) copy-start(bf16[32,48,224]{2,1,0:T(8,128)(2,1)} %mid_ref) | copy-start | bytes 2064388
  1.8 8.5 %copy-start.1 = (bf16[32,48,224]{2,1,0:T(8,128)(2,1)S(1)}, bf16[32,48,224]{2,1,0:T(8,128)(2,1)}, u32[]{:S(2)}) copy-start(bf16[32,48,224]{2,1,0:T(8,128)(2,1)} %mid_ref) | copy-start | bytes 2064388
  2.9 15.0 %all-to-all-start = ((f32[32,1,896]{2,1,0:T(1,128)}), f32[32,1,896]{2,1,0:T(1,128)S(1)}, u32[]{:S(2)}, u32[]{:S(2)}) async-start(f32[32,1,896]{2,1,0:T(1,128)} %bitcast), calls=%async_computation | async-start | bytes 229376 | tf_op jit(solution)/shard_map/all_to_all | solution.py:355
  10.3 12.4 %collective-permute-start.1 = (bf16[32,3,224]{2,1,0:T(4,128)(2,1)S(1)}, bf16[32,3,224]{2,1,0:T(4,128)(2,1)S(1)}, u32[]{:S(2)}, u32[]{:S(2)}) collective-permute-start(bf16[32,3,224]{2,1,0:T(4,128)(2,1)S(1)} %get-tuple-element.14), channel_id=1, source_target_pairs={{4,0},{8,4},{12,8},{16,12},{20,16},{24,20},{28,24},{5,1},{9,5},{13... | collective-permute-start | bytes 129032 | tf_op jit(solution)/shard_map/ppermute | solution.py:350
  11.6 11.1 %collective-permute-start = (bf16[32,3,224]{2,1,0:T(4,128)(2,1)S(1)}, bf16[32,3,224]{2,1,0:T(4,128)(2,1)S(1)}, u32[]{:S(2)}, u32[]{:S(2)}) collective-permute-start(bf16[32,3,224]{2,1,0:T(4,128)(2,1)S(1)} %get-tuple-element.15), channel_id=1, source_target_pairs={{0,4},{4,8},{8,12},{12,16},{16,20},{20,24},{24,28},{1,5},{5,9},{9,... | collective-permute-start | bytes 129032 | tf_op jit(solution)/shard_map/ppermute | solution.py:349
  18.6 11.7 %all-to-all-start.1 = ((f32[32,1,896]{2,1,0:T(1,128)}), f32[32,1,896]{2,1,0:T(1,128)S(1)}, u32[]{:S(2)}, u32[]{:S(2)}) async-start(f32[32,1,896]{2,1,0:T(1,128)} %bitcast.2), calls=%async_computation.1 | async-start | bytes 229376 | tf_op jit(solution)/shard_map/all_to_all | solution.py:355
  22.7 7.6 %copy-start.2 = (f32[16,256]{1,0:T(8,128)S(1)}, f32[16,256]{1,0:T(8,128)}, u32[]{:S(2)}) copy-start(f32[16,256]{1,0:T(8,128)} %constant.2.clone.start_ref) | copy-start | bytes 49156
  22.8 9.8 %collective-permute-start.2 = (bf16[3,56,224]{2,1,0:T(8,128)(2,1)S(1)}, bf16[3,56,224]{2,1,0:T(8,128)(2,1)S(1)}, u32[]{:S(2)}, u32[]{:S(2)}) collective-permute-start(bf16[3,56,224]{2,1,0:T(8,128)(2,1)S(1)} %get-tuple-element.9), channel_id=1, source_target_pairs={{0,1},{1,2},{2,3},{4,5},{5,6},{6,7},{8,9},{9,10},{10,11},{12,13},{... | collective-permute-start | bytes 225800 | tf_op jit(solution)/shard_map/ppermute | solution.py:403
  24.9 7.7 %collective-permute-start.3 = (bf16[3,56,224]{2,1,0:T(8,128)(2,1)S(1)}, bf16[3,56,224]{2,1,0:T(8,128)(2,1)S(1)}, u32[]{:S(2)}, u32[]{:S(2)}) collective-permute-start(bf16[3,56,224]{2,1,0:T(8,128)(2,1)S(1)} %get-tuple-element.10), channel_id=1, source_target_pairs={{1,0},{2,1},{3,2},{5,4},{6,5},{7,6},{9,8},{10,9},{11,10},{13,12},{... | collective-permute-start | bytes 225800 | tf_op jit(solution)/shard_map/ppermute | solution.py:404

commit v6 on v5

--- a/solution.py
+++ b/solution.py
@@ -278,7 +278,7 @@
         while ready < len(groups) and groups[ready][0] <= r + 1 + AHEAD:
             fit_rows(*groups[ready])
             ready += 1
-            if ready == 4:
+            if ready == len(groups):
                 project()
         for h in range(len(lanes)):
             now = natural(fit, h, r)

time: 37.6 us -> 37.6 us (level)
  no operation moved by 1% of the time
where the time goes in v6:
time: 37.6 us; the launch traced here: 37.2 us
  starting transfers between devices  20.7 us (55%)
  Pallas kernels  8.83 us (23%)
  waiting for transfers between devices  5.77 us (15%)
  local copies, waits for them, and re-layouts  1.2 us (3%)
  between operations  0.76 us (2%)
    all_to_all x2, starting transfers between devices, exchange(): return lax.all_to_all(pieces, axes, split_axis=0, concat_axis=0)  11.4 us
    all_to_all x2, waiting for transfers between devices, exchange(): return lax.all_to_all(pieces, axes, split_axis=0, concat_axis=0)  5.76 us
    pallas_call x1, Pallas kernels, body(): pl.pallas_call(functools.partial(main_kernel, depth, n_rows, n_cols), in_...  4.64 us
    ppermute x1, starting transfers between devices, neighbours(): before = lax.ppermute(tail, axis, [(i, i + 1) for i in range(count - 1)])  4.55 us
    pallas_call x1, Pallas kernels, body(): pl.pallas_call(functools.partial(subspace_kernel, inv_count), in_specs=[v...  2.27 us
    ppermute x1, starting transfers between devices, body(): lax.ppermute(down, 'narrow', [(i, i + 1) for i in range(n_rows - 1)])  2.16 us
    ppermute x1, starting transfers between devices, body(): below = lax.ppermute(up, 'narrow', [(i + 1, i) for i in range(n_rows - 1)])  1.29 us
    ppermute x1, starting transfers between devices, neighbours(): after = lax.ppermute(head, axis, [(i + 1, i) for i in range(count - 1)])  1.29 us
  transfers between devices with their start and end apart: 6, of which 2 were waited for; matrix products, arithmetic and copies ran while one was open for 0% of the time, Pallas kernels for 8%

profile of v6, /device:TPU:0, one launch (start us, length us, event | category | flops | bytes accessed | tf_op | source)
XLA Modules:
  0.0 37.2 jit_solution(911864541662923070)
XLA Ops:
  0.6 0.0 copy-start
  0.6 1.1 %copy-done = bf16[32,48,224]{2,1,0:T(8,128)(2,1)S(1)} copy-done((bf16[32,48,224]{2,1,0:T(8,128)(2,1)S(1)}, bf16[32,48,224]{2,1,0:T(8,128)(2,1)}, u32[]{:S(2)}) %copy-start) | copy-done | bytes 688152
  1.8 0.0 copy-start.1
  1.8 1.2 %shard_map.41 = f32[224,128]{1,0:T(8,128)} custom-call(bf16[32,48,224]{2,1,0:T(8,128)(2,1)S(1)} %copy-done), custom_call_target="tpu_custom_call" | custom-call | tf_op jit(solution)/shard_map/pallas_call | solution.py:368
  2.9 7.3 %all-to-all-start = ((f32[32,1,896]{2,1,0:T(1,128)}), f32[32,1,896]{2,1,0:T(1,128)S(1)}, u32[]{:S(2)}, u32[]{:S(2)}) async-start(f32[32,1,896]{2,1,0:T(1,128)} %bitcast), calls=%async_computation | async-start | bytes 229376 | tf_op jit(solution)/shard_map/all_to_all | solution.py:355
  10.2 0.0 copy-done.1
  10.2 0.1 fusion.1
  10.3 1.3 %collective-permute-start.1 = (bf16[32,3,224]{2,1,0:T(4,128)(2,1)S(1)}, bf16[32,3,224]{2,1,0:T(4,128)(2,1)S(1)}, u32[]{:S(2)}, u32[]{:S(2)}) collective-permute-start(bf16[32,3,224]{2,1,0:T(4,128)(2,1)S(1)} %get-tuple-element.14), channel_id=1, source_target_pairs={{4,0},{8,4},{12,8},{16,12},{20,16},{24,20},{28,24},{5,1},{9,5},{13... | collective-permute-start | bytes 129032 | tf_op jit(solution)/shard_map/ppermute | solution.py:350
  11.6 4.5 %collective-permute-start = (bf16[32,3,224]{2,1,0:T(4,128)(2,1)S(1)}, bf16[32,3,224]{2,1,0:T(4,128)(2,1)S(1)}, u32[]{:S(2)}, u32[]{:S(2)}) collective-permute-start(bf16[32,3,224]{2,1,0:T(4,128)(2,1)S(1)} %get-tuple-element.15), channel_id=1, source_target_pairs={{0,4},{4,8},{8,12},{12,16},{16,20},{20,24},{24,28},{1,5},{5,9},{9,... | collective-permute-start | bytes 129032 | tf_op jit(solution)/shard_map/ppermute | solution.py:349
  16.2 1.7 %all-to-all-done = f32[32,1,896]{2,1,0:T(1,128)S(1)} async-done(((f32[32,1,896]{2,1,0:T(1,128)}), f32[32,1,896]{2,1,0:T(1,128)S(1)}, u32[]{:S(2)}, u32[]{:S(2)}) %all-to-all-start) | async-done | bytes 114720 | tf_op jit(solution)/shard_map/all_to_all | solution.py:355
  17.9 0.7 %shard_map.42 = f32[224,128]{1,0:T(8,128)} custom-call(f32[224,128]{1,0:T(8,128)S(1)} %bitcast.4), custom_call_target="tpu_custom_call" | custom-call | tf_op jit(solution)/shard_map/pallas_call | solution.py:380
  18.6 4.1 %all-to-all-start.1 = ((f32[32,1,896]{2,1,0:T(1,128)}), f32[32,1,896]{2,1,0:T(1,128)S(1)}, u32[]{:S(2)}, u32[]{:S(2)}) async-start(f32[32,1,896]{2,1,0:T(1,128)} %bitcast.2), calls=%async_computation.1 | async-start | bytes 229376 | tf_op jit(solution)/shard_map/all_to_all | solution.py:355
  22.7 0.0 collective-permute-done.1.right_ref
  22.7 0.0 collective-permute-done.left_ref
  22.7 0.0 copy-start.2
  22.7 0.1 shard_map.44
  22.8 2.2 %collective-permute-start.2 = (bf16[3,56,224]{2,1,0:T(8,128)(2,1)S(1)}, bf16[3,56,224]{2,1,0:T(8,128)(2,1)S(1)}, u32[]{:S(2)}, u32[]{:S(2)}) collective-permute-start(bf16[3,56,224]{2,1,0:T(8,128)(2,1)S(1)} %get-tuple-element.9), channel_id=1, source_target_pairs={{0,1},{1,2},{2,3},{4,5},{5,6},{6,7},{8,9},{9,10},{10,11},{12,13},{... | collective-permute-start | bytes 225800 | tf_op jit(solution)/shard_map/ppermute | solution.py:403
  24.9 1.3 %collective-permute-start.3 = (bf16[3,56,224]{2,1,0:T(8,128)(2,1)S(1)}, bf16[3,56,224]{2,1,0:T(8,128)(2,1)S(1)}, u32[]{:S(2)}, u32[]{:S(2)}) collective-permute-start(bf16[3,56,224]{2,1,0:T(8,128)(2,1)S(1)} %get-tuple-element.10), channel_id=1, source_target_pairs={{1,0},{2,1},{3,2},{5,4},{6,5},{7,6},{9,8},{10,9},{11,10},{13,12},{... | collective-permute-start | bytes 225800 | tf_op jit(solution)/shard_map/ppermute | solution.py:404
  26.2 4.1 %all-to-all-done.1 = f32[32,1,896]{2,1,0:T(1,128)S(1)} async-done(((f32[32,1,896]{2,1,0:T(1,128)}), f32[32,1,896]{2,1,0:T(1,128)S(1)}, u32[]{:S(2)}, u32[]{:S(2)}) %all-to-all-start.1) | async-done | bytes 114720 | tf_op jit(solution)/shard_map/all_to_all | solution.py:355
  30.3 0.0 copy-done.2
  30.3 2.3 %shard_map.43.basis_ref = f32[16,256]{1,0:T(8,128)S(1)} custom-call(f32[224,128]{1,0:T(8,128)S(1)} %bitcast.5, f32[16,256]{1,0:T(8,128)S(1)} %copy-done.2), custom_call_target="tpu_custom_call" | custom-call | flops 4294967296 | bytes 262144 | tf_op jit(solution)/shard_map/pallas_call | solution.py:407
  32.6 0.0 collective-permute-done.2.above_ref
  32.6 0.0 collective-permute-done.3.below_ref
  32.6 4.6 %shard_map.45 = (bf16[32,48,224]{2,1,0:T(8,128)(2,1)}, f32[224,224]{1,0:T(8,128)}) custom-call(f32[16,256]{1,0:T(8,128)S(1)} %shard_map.43.basis_ref, bf16[32,48,224]{2,1,0:T(8,128)(2,1)S(1)} %copy-done.1, bf16[3,56,224]{2,1,0:T(8,128)(2,1)S(1)} %collective-permute-done.2.above_ref, bf16[3,56,224]{2,1,0:T(8,128)(2,1)S(1)} %collective-permute-done.3.below_ref, ...), custom_call_target="tpu_custom_call" | custom-call | tf_op jit(solution)/shard_map/pallas_call | solution.py:416
  (1 shorter events, 0.0 us)
Async XLA Ops:
  0.6 1.1 %copy-start = (bf16[32,48,224]{2,1,0:T(8,128)(2,1)S(1)}, bf16[32,48,224]{2,1,0:T(8,128)(2,1)}, u32[]{:S(2)}) copy-start(bf16[32,48,224]{2,1,0:T(8,128)(2,1)} %mid_ref) | copy-start | bytes 2064388
  1.8 8.5 %copy-start.1 = (bf16[32,48,224]{2,1,0:T(8,128)(2,1)S(1)}, bf16[32,48,224]{2,1,0:T(8,128)(2,1)}, u32[]{:S(2)}) copy-start(bf16[32,48,224]{2,1,0:T(8,128)(2,1)} %mid_ref) | copy-start | bytes 2064388
  2.9 15.0 %all-to-all-start = ((f32[32,1,896]{2,1,0:T(1,128)}), f32[32,1,896]{2,1,0:T(1,128)S(1)}, u32[]{:S(2)}, u32[]{:S(2)}) async-start(f32[32,1,896]{2,1,0:T(1,128)} %bitcast), calls=%async_computation | async-start | bytes 229376 | tf_op jit(solution)/shard_map/all_to_all | solution.py:355
  10.3 12.4 %collective-permute-start.1 = (bf16[32,3,224]{2,1,0:T(4,128)(2,1)S(1)}, bf16[32,3,224]{2,1,0:T(4,128)(2,1)S(1)}, u32[]{:S(2)}, u32[]{:S(2)}) collective-permute-start(bf16[32,3,224]{2,1,0:T(4,128)(2,1)S(1)} %get-tuple-element.14), channel_id=1, source_target_pairs={{4,0},{8,4},{12,8},{16,12},{20,16},{24,20},{28,24},{5,1},{9,5},{13... | collective-permute-start | bytes 129032 | tf_op jit(solution)/shard_map/ppermute | solution.py:350
  11.6 11.1 %collective-permute-start = (bf16[32,3,224]{2,1,0:T(4,128)(2,1)S(1)}, bf16[32,3,224]{2,1,0:T(4,128)(2,1)S(1)}, u32[]{:S(2)}, u32[]{:S(2)}) collective-permute-start(bf16[32,3,224]{2,1,0:T(4,128)(2,1)S(1)} %get-tuple-element.15), channel_id=1, source_target_pairs={{0,4},{4,8},{8,12},{12,16},{16,20},{20,24},{24,28},{1,5},{5,9},{9,... | collective-permute-start | bytes 129032 | tf_op jit(solution)/shard_map/ppermute | solution.py:349
  18.6 11.7 %all-to-all-start.1 = ((f32[32,1,896]{2,1,0:T(1,128)}), f32[32,1,896]{2,1,0:T(1,128)S(1)}, u32[]{:S(2)}, u32[]{:S(2)}) async-start(f32[32,1,896]{2,1,0:T(1,128)} %bitcast.2), calls=%async_computation.1 | async-start | bytes 229376 | tf_op jit(solution)/shard_map/all_to_all | solution.py:355
  22.7 7.6 %copy-start.2 = (f32[16,256]{1,0:T(8,128)S(1)}, f32[16,256]{1,0:T(8,128)}, u32[]{:S(2)}) copy-start(f32[16,256]{1,0:T(8,128)} %constant.2.clone.start_ref) | copy-start | bytes 49156
  22.8 9.8 %collective-permute-start.2 = (bf16[3,56,224]{2,1,0:T(8,128)(2,1)S(1)}, bf16[3,56,224]{2,1,0:T(8,128)(2,1)S(1)}, u32[]{:S(2)}, u32[]{:S(2)}) collective-permute-start(bf16[3,56,224]{2,1,0:T(8,128)(2,1)S(1)} %get-tuple-element.9), channel_id=1, source_target_pairs={{0,1},{1,2},{2,3},{4,5},{5,6},{6,7},{8,9},{9,10},{10,11},{12,13},{... | collective-permute-start | bytes 225800 | tf_op jit(solution)/shard_map/ppermute | solution.py:403
  24.9 7.7 %collective-permute-start.3 = (bf16[3,56,224]{2,1,0:T(8,128)(2,1)S(1)}, bf16[3,56,224]{2,1,0:T(8,128)(2,1)S(1)}, u32[]{:S(2)}, u32[]{:S(2)}) collective-permute-start(bf16[3,56,224]{2,1,0:T(8,128)(2,1)S(1)} %get-tuple-element.10), channel_id=1, source_target_pairs={{1,0},{2,1},{3,2},{5,4},{6,5},{7,6},{9,8},{10,9},{11,10},{13,12},{... | collective-permute-start | bytes 225800 | tf_op jit(solution)/shard_map/ppermute | solution.py:404
